TPU v7x, 512 devices: a whole 4x4x16 slice. The times are simulated.
512 devices in a mesh: grp: 16 (over z), dev: 32 (over y, x, core).
Axes of the slice: x: 4, y: 4, z: 16, core: 2. Of those that a mesh axis runs over, the one named last changes fastest.
Arguments:
- signals: bfloat16 [192, 96, 256, 256], P(None, 'grp', 'dev'), may hold values from -17 to 17
- tile_flags: int32 [96, 256, 2], P('grp', 'dev'), may hold values 0 or 1
- basis_old: float32 [192, 8], replicated, may hold values from -6 to 6
- tv_weight: float32 [96, 256, 256], P('grp', 'dev'), may hold values from 0.2 to 2
Outputs:
- basis: float32 [192, 8], replicated
- coefficients: float32 [8, 96, 256, 256], P(None, 'grp', 'dev')
All inputs are finite; a program needn't handle non-finite values. No bound on the sum of `tile_flags` on one device may be relied on, other than what follows from the above.
Results may differ from a plain program's by a relative error of at most 0.002.
Values sent between devices are 32-bit elements; how exact they have to be, the bound alone decides.
No kernel may reach another device: no remote copies, remote signals or barrier semaphores. Data moves between devices by JAX's collectives and lax.ppermute only.
A program may use at most 64 MiB of HBM per device.

v0:
```python
import jax
import jax.numpy as jnp
from jax import lax
from jax.sharding import PartitionSpec as P

step_size = 0.08


def padded(cells, sides, width):
    for axis, dim in sides:
        count = lax.axis_size(axis)
        ends = count - 1
        head = lax.slice_in_dim(cells, 0, width, axis=dim)
        tail = lax.slice_in_dim(cells, cells.shape[dim] - width, cells.shape[dim], axis=dim)
        cells = jnp.concatenate(
            [
                lax.ppermute(tail, axis, [(i, (i + 1) % count) for i in range(ends)]),
                cells,
                lax.ppermute(head, axis, [((i + 1) % count, i) for i in range(ends)]),
            ],
            axis=dim,
        )
    return cells


def tv_update(extended, weight):
    zpad = jnp.pad(extended, ((0, 0), (0, 0), (0, 0), (1, 1)))
    center = zpad[:, 1:-1, 1:-1, 1:-1]
    neighbours = [
        zpad[:, 2:, 1:-1, 1:-1],
        zpad[:, :-2, 1:-1, 1:-1],
        zpad[:, 1:-1, 2:, 1:-1],
        zpad[:, 1:-1, :-2, 1:-1],
        zpad[:, 1:-1, 1:-1, 2:],
        zpad[:, 1:-1, 1:-1, :-2],
    ]
    total = jnp.zeros_like(center)
    for other in neighbours:
        diff = other - center
        total = total + diff / jnp.sqrt(1.0 + diff * diff)
    return center + step_size * weight * total


def orthonormal(grown):
    small = jnp.dot(grown.T, grown, precision=lax.Precision.HIGHEST)
    lower = jnp.linalg.cholesky(small)
    return lax.linalg.triangular_solve(lower, grown, left_side=False, lower=True, transpose_a=True)


def split_pair(values):
    upper = values.astype(jnp.bfloat16)
    rest = (values - upper.astype(jnp.float32)).astype(jnp.bfloat16)
    return (upper, rest)


def left_apply(matrix_t, flat):
    upper, rest = split_pair(matrix_t)
    return jnp.dot(upper, flat, preferred_element_type=jnp.float32) + jnp.dot(
        rest, flat, preferred_element_type=jnp.float32
    )


def on_device(signals, tile_flags, basis_old, tv_weight):
    frames, size_x, size_y, size_z = signals.shape
    tiles = tile_flags.shape[2]
    width = size_z // tiles
    flags = tile_flags.astype(jnp.bfloat16)[None, :, :, :, None]
    masked = (signals.reshape(frames, size_x, size_y, tiles, width) * flags).reshape(frames, -1)
    local_gram = lax.dot_general(
        masked, masked, (((1,), (1,)), ((), ())), preferred_element_type=jnp.float32
    )
    gram = lax.psum(local_gram, ("grp", "dev"))
    grown = jnp.dot(gram, basis_old, precision=lax.Precision.HIGHEST)
    basis = orthonormal(grown)
    rank = basis.shape[1]
    coef = left_apply(basis.T, masked).reshape(rank, size_x, size_y, size_z)
    for sweep in range(2):
        extended = padded(coef, (("grp", 1), ("dev", 2)), 1)
        coef = tv_update(extended, tv_weight)
    return (basis, coef)


def solution(mesh):
    placed = (P(None, "grp", "dev", None), P("grp", "dev", None), P(), P("grp", "dev", None))
    return jax.shard_map(
        on_device,
        mesh=mesh,
        in_specs=placed,
        out_specs=(P(), P(None, "grp", "dev", None)),
        check_vma=False,
    )
```

profile of v0, /device:TPU:1, one launch (start us, length us, event | category | flops | bytes accessed | tf_op | source)
XLA Modules:
  0.0 524.8 jit_solution(207497487192355755)
XLA Ops:
  7.2 0.7 convert_element_type.15
  8.2 2.7 broadcast_multiply_fusion
  10.9 4.4 fusion.8
  15.3 6.6 %copy.37 = bf16[24,8,48,256]{3,1,2,0:T(8,128)(2,1)} copy(bf16[24,8,48,256]{3,2,1,0:T(8,128)(2,1)} %bitcast.45) | data formatting | bytes 9437184
  21.9 453.6 %all-reduce.4.cloned.1.call-done = f32[192,192]{1,0:T(8,128)} async-done(((f32[192,192]{1,0:T(8,128)}), f32[192,192]{1,0:T(8,128)}) %all-reduce.4.cloned.1.call-update) | async-done | bytes 147472 | tf_op jit(solution)/shard_map/psum | solution.py:72
  475.5 1.1 fusion.31
  479.8 3.2 fusion.3
  483.6 0.7 convolution_add_fusion
  484.5 1.3 collective-permute-start.1
  485.8 1.3 collective-permute-start
  487.6 3.8 collective-permute-done
  491.4 2.8 collective-permute-start.2
  494.2 3.0 collective-permute-start.3
  497.2 1.3 collective-permute-done.3
  498.5 1.0 select_maximum_fusion.4
  499.5 0.7 multiply_add_fusion.1
  500.2 1.3 collective-permute-start.4
  501.5 4.0 collective-permute-start.5
  505.5 1.6 collective-permute-done.5
  507.2 2.0 collective-permute-start.6
  509.3 5.0 collective-permute-start.7
  514.3 1.3 collective-permute-done.7
  515.6 1.0 select_maximum_fusion
  516.5 1.4 multiply_add_fusion
  (35 shorter events, 4.8 us)
Async XLA Ops:
  7.2 468.3 %copy-start = (f32[192,8]{0,1:T(8,128)S(1)}, f32[192,8]{0,1:T(8,128)}, u32[]{:S(2)}) copy-start(f32[192,8]{0,1:T(8,128)} %param.6) | copy-start | bytes 18436
  7.2 468.3 %all-reduce.4.cloned.1.call-start = ((), (), s32[]{:S(2)}) async-start(), calls=%async_computation | async-start | bytes 393216 | tf_op jit(solution)/shard_map/psum | solution.py:72
  479.8 3.2 copy-start.3
  479.8 3.8 copy-start.1
  484.3 12.9 %copy-start.2 = (f32[6,8,256]{2,1,0:T(8,128)S(1)}, f32[6,8,256]{2,1,0:T(8,128)}, u32[]{:S(2)}) copy-start(f32[6,8,256]{2,1,0:T(8,128)} %param.7) | copy-start | bytes 147460
  484.5 3.0 collective-permute-start.1
  485.8 5.6 %collective-permute-start = (f32[8,1,8,256]{3,2,1,0:T(8,128)S(1)}, f32[8,1,8,256]{3,2,1,0:T(8,128)S(1)}, u32[]{:S(2)}, u32[]{:S(2)}) collective-permute-start(f32[8,1,8,256]{3,2,1,0:T(8,128)S(1)} %get-tuple-element.8), channel_id=1, source_target_pairs={{32,0},{64,32},{96,64},{128,96},{160,128},{192,160},{224,192},{256... | collective-permute-start | bytes 196616 | tf_op jit(solution)/shard_map/ppermute | solution.py:19
  491.4 5.8 %collective-permute-start.2 = (f32[8,8,1,256]{3,2,1,0:T(1,128)S(1)}, f32[8,8,1,256]{3,2,1,0:T(1,128)S(1)}, u32[]{:S(2)}, u32[]{:S(2)}) collective-permute-start(f32[8,8,1,256]{3,2,1,0:T(1,128)S(1)} %get-tuple-element.5), channel_id=1, source_target_pairs={{1,0},{2,1},{3,2},{4,3},{5,4},{6,5},{7,6},{8,7},{9,8},{10,9},{11,1... | collective-permute-start | bytes 196616 | tf_op jit(solution)/shard_map/ppermute | solution.py:19
  494.2 4.3 collective-permute-start.3
  500.2 5.3 %collective-permute-start.4 = (f32[8,1,8,256]{3,2,1,0:T(8,128)S(1)}, f32[8,1,8,256]{3,2,1,0:T(8,128)S(1)}, u32[]{:S(2)}, u32[]{:S(2)}) collective-permute-start(f32[8,1,8,256]{3,2,1,0:T(8,128)S(1)} %get-tuple-element.7), channel_id=1, source_target_pairs={{32,0},{64,32},{96,64},{128,96},{160,128},{192,160},{224,192},{256... | collective-permute-start | bytes 196616 | tf_op jit(solution)/shard_map/ppermute | solution.py:19
  501.5 5.6 %collective-permute-start.5 = (f32[8,1,8,256]{3,2,1,0:T(8,128)S(1)}, f32[8,1,8,256]{3,2,1,0:T(8,128)S(1)}, u32[]{:S(2)}, u32[]{:S(2)}) collective-permute-start(f32[8,1,8,256]{3,2,1,0:T(8,128)S(1)} %get-tuple-element.6), channel_id=1, source_target_pairs={{0,32},{32,64},{64,96},{96,128},{128,160},{160,192},{192,224},{224... | collective-permute-start | bytes 196616 | tf_op jit(solution)/shard_map/ppermute | solution.py:17
  507.2 7.0 %collective-permute-start.6 = (f32[8,8,1,256]{3,2,1,0:T(1,128)S(1)}, f32[8,8,1,256]{3,2,1,0:T(1,128)S(1)}, u32[]{:S(2)}, u32[]{:S(2)}) collective-permute-start(f32[8,8,1,256]{3,2,1,0:T(1,128)S(1)} %get-tuple-element.3), channel_id=1, source_target_pairs={{1,0},{2,1},{3,2},{4,3},{5,4},{6,5},{7,6},{8,7},{9,8},{10,9},{11,1... | collective-permute-start | bytes 196616 | tf_op jit(solution)/shard_map/ppermute | solution.py:19
  509.3 6.3 %collective-permute-start.7 = (f32[8,8,1,256]{3,2,1,0:T(1,128)S(1)}, f32[8,8,1,256]{3,2,1,0:T(1,128)S(1)}, u32[]{:S(2)}, u32[]{:S(2)}) collective-permute-start(f32[8,8,1,256]{3,2,1,0:T(1,128)S(1)} %get-tuple-element.2), channel_id=1, source_target_pairs={{0,1},{1,2},{2,3},{3,4},{4,5},{5,6},{6,7},{7,8},{8,9},{9,10},{10,1... | collective-permute-start | bytes 196616 | tf_op jit(solution)/shard_map/ppermute | solution.py:17
Sparse Core Ops, SparseCore 0:
  15.5 460.0 all-reduce.3
where the time goes:
time: 531 us; the launch traced here: 525 us
  waiting for transfers between devices  462 us (87%)
  starting transfers between devices  20.7 us (4%)
  between operations  14.2 us (3%)
  other arithmetic  10.2 us (2%)
  matrix products  9.92 us (2%)
  local copies, waits for them, and re-layouts  7.84 us (1%)
    psum x1, waiting for transfers between devices, on_device(): gram = lax.psum(local_gram, ('grp', 'dev'))  454 us
    ppermute x4, starting transfers between devices, padded(): lax.ppermute(tail, axis, [(i, (i + 1) % count) for i in range(ends)])  13.3 us
  transfers between devices with their start and end apart: 9, of which 6 were waited for; matrix products, arithmetic and copies ran while one was open for 1% of the time, Pallas kernels for 0%

commit v1 on v0

v1 whole, which is shorter than its diff:
```python
import functools

import jax
import jax.numpy as jnp
import numpy as np
from jax import lax
from jax.experimental import pallas as pl
from jax.experimental.pallas import tpu as pltpu
from jax.sharding import PartitionSpec as P

step_size = 0.08
limit = 40 * 1024 * 1024
NT = (((1,), (1,)), ((), ()))
TN = (((0,), (0,)), ((), ()))


def dot(a, b, dims=(((1,), (0,)), ((), ()))):
    return lax.dot_general(a, b, dims, preferred_element_type=jnp.float32)


def terms(values, count):
    parts = []
    for _ in range(count):
        part = values.astype(jnp.bfloat16)
        parts.append(part)
        values = values - part.astype(jnp.float32)
    return parts


def spread_rows(repeated, rows):
    lane = lax.broadcasted_iota(jnp.int32, repeated.shape, 1) % rows
    return [jnp.where(lane == y, repeated, 0.0) for y in range(rows)]


def to_dense(values):
    rest = values[:, 128:]
    tail = jnp.concatenate([rest[:4], rest[4:]], axis=1)
    return jnp.stack([values[:4, :128], values[4:, :128], tail])


def from_dense(values):
    first = jnp.concatenate([values[0], values[1]], axis=0)
    rest = jnp.concatenate([values[2, :, :64], values[2, :, 64:]], axis=0)
    return jnp.concatenate([first, rest], axis=1)


def tile_mask(flags, width, tiles):
    return jnp.concatenate([jnp.broadcast_to(flags[:, t : t + 1], (flags.shape[0], width)) for t in range(tiles)], axis=1)


def load_planes(signals, planes, sems):
    copies = [
        pltpu.make_async_copy(signals.at[:, i], planes.at[i], sems.at[i]) for i in range(planes.shape[0])
    ]
    for copy in copies:
        copy.start()
    return copies


def rows_of(plane):
    frames, rows, width = plane.shape
    return plane.astype(jnp.float32).reshape(frames * rows, width).astype(jnp.bfloat16)


def grown_kernel(signals, flags, basis_old, select, out, planes, sems):
    copies = load_planes(signals, planes, sems)
    count, frames, rows, width = planes.shape
    rank = basis_old.shape[1]
    spread = []
    for part in terms(basis_old[...], 3):
        spread += spread_rows(dot(part, select[...], TN), rows)
    weights = jnp.concatenate(spread, axis=0).astype(jnp.bfloat16)
    total = jnp.zeros((rows * rank, frames * rows), jnp.float32)
    for i in range(count):
        copies[i].wait()
        flat = rows_of(planes[i])
        mixed = dot(weights, flat).reshape(3, rows * rank, width).sum(0)
        keep = tile_mask(flags[i].astype(jnp.float32), width // flags.shape[2], flags.shape[2])
        mixed = (mixed.reshape(rows, rank, width) * keep[:, None, :]).reshape(rows * rank, width)
        product = dot(jnp.concatenate(terms(mixed, 3), axis=0), flat, NT)
        total = total + product.reshape(3, rows * rank, frames * rows).sum(0)
    total = total.reshape(rows, rank, frames * rows)
    lane = lax.broadcasted_iota(jnp.int32, (rank, frames * rows), 1) % rows
    diagonal = jnp.zeros((rank, frames * rows), jnp.float32)
    for y in range(rows):
        diagonal = diagonal + jnp.where(lane == y, total[y], 0.0)
    grown = dot(jnp.concatenate(terms(diagonal, 3), axis=0), select[...], NT)
    grown = grown.reshape(3, rank, frames).sum(0)
    out[...] = jnp.broadcast_to(to_dense(grown)[None], out.shape)


def local_grown(signals, tile_flags, basis_old, select, copies):
    frames, size_x, size_y, size_z = signals.shape
    return pl.pallas_call(
        grown_kernel,
        out_shape=jax.ShapeDtypeStruct((copies, 3, 4, 128), jnp.float32),
        in_specs=[pl.BlockSpec(memory_space=pl.ANY)] + [pl.BlockSpec(memory_space=pltpu.VMEM)] * 3,
        out_specs=pl.BlockSpec(memory_space=pltpu.VMEM),
        scratch_shapes=[
            pltpu.VMEM((size_x, frames, size_y, size_z), signals.dtype),
            pltpu.SemaphoreType.DMA((size_x,)),
        ],
        compiler_params=pltpu.CompilerParams(vmem_limit_bytes=limit),
        name="local_grown",
    )(signals, tile_flags, basis_old, select)


def resend_kernel(parts, out):
    out[...] = jnp.broadcast_to(jnp.sum(parts[...], axis=0, keepdims=True), out.shape)


def sum_and_copy(parts, copies):
    return pl.pallas_call(
        resend_kernel,
        out_shape=jax.ShapeDtypeStruct((copies,) + parts.shape[1:], jnp.float32),
        in_specs=[pl.BlockSpec(memory_space=pltpu.VMEM)],
        out_specs=pl.BlockSpec(memory_space=pltpu.VMEM),
        name="sum_and_copy",
    )(parts)


def orthonormal(grown):
    rank = grown.shape[0]
    row = lax.broadcasted_iota(jnp.int32, (rank, 1), 0)
    for k in range(rank):
        pivot = grown[k : k + 1]
        inner = jnp.sum(grown * pivot, axis=1, keepdims=True)
        norm2 = inner[k : k + 1]
        scaled = pivot * (1.0 / norm2)
        grown = jnp.where(row > k, grown - inner * scaled, grown)
        grown = jnp.where(row == k, pivot / jnp.sqrt(norm2), grown)
    return grown


def project_kernel(parts, signals, flags, select, weight, basis_out, coef, head, tail, planes, sems):
    copies = load_planes(signals, planes, sems)
    count, frames, rows, width = planes.shape
    basis = orthonormal(from_dense(jnp.sum(parts[...], axis=0)))
    rank = basis.shape[0]
    basis_out[...] = basis
    spread = []
    for part in terms(basis, 2):
        spread += spread_rows(dot(part, select[...]), rows)
    weights = jnp.concatenate(spread, axis=0).astype(jnp.bfloat16)
    for i in range(count):
        copies[i].wait()
        mixed = dot(weights, rows_of(planes[i])).reshape(2, rows, rank, width).sum(0)
        keep = tile_mask(flags[i].astype(jnp.float32), width // flags.shape[2], flags.shape[2])
        mixed = mixed * keep[:, None, :]
        coef[i] = mixed
        for y in range(2):
            head[y * count + i] = mixed[y]
            tail[y * count + i] = mixed[rows - 2 + y]
    head[2 * count, :count] = weight[:, 0]
    tail[2 * count, :count] = weight[:, rows - 1]
    head[2 * count, count:] = jnp.zeros((rank - count, width), jnp.float32)
    tail[2 * count, count:] = jnp.zeros((rank - count, width), jnp.float32)


def project(parts, signals, tile_flags, select, tv_weight, rank):
    frames, size_x, size_y, size_z = signals.shape
    edge = jax.ShapeDtypeStruct((2 * size_x + 1, rank, size_z), jnp.float32)
    vmem = pl.BlockSpec(memory_space=pltpu.VMEM)
    return pl.pallas_call(
        project_kernel,
        out_shape=(
            jax.ShapeDtypeStruct((rank, frames), jnp.float32),
            jax.ShapeDtypeStruct((size_x, size_y, rank, size_z), jnp.float32),
            edge,
            edge,
        ),
        in_specs=[vmem, pl.BlockSpec(memory_space=pl.ANY), vmem, vmem, vmem],
        out_specs=(vmem,) * 4,
        scratch_shapes=[
            pltpu.VMEM((size_x, frames, size_y, size_z), signals.dtype),
            pltpu.SemaphoreType.DMA((size_x,)),
        ],
        compiler_params=pltpu.CompilerParams(vmem_limit_bytes=limit),
        name="project",
    )(parts, signals, tile_flags, select, tv_weight)


def slope(diff):
    return diff * lax.rsqrt(1.0 + diff * diff)


def along_z(cells):
    width = cells.shape[-1]
    lane = lax.broadcasted_iota(jnp.int32, cells.shape, cells.ndim - 1)
    above = jnp.where(lane == width - 1, 0.0, pltpu.roll(cells, width - 1, cells.ndim - 1))
    flux = slope(above - cells)
    below = jnp.where(lane == 0, slope(cells), pltpu.roll(flux, 1, cells.ndim - 1))
    return flux - below


def smooth_kernel(coef, left, right, down, up, weight, out, first, second, weights):
    count, rows, rank, width = coef.shape
    planes = count + 4
    lo, hi = slice(2, 2 + rows), slice(1, 3 + rows)
    first[0, lo] = down[:rows]
    first[1, hi] = down[rows : 2 * rows + 2]
    first[planes - 1, lo] = up[:rows]
    first[planes - 2, hi] = up[rows : 2 * rows + 2]
    first[2 : 2 + count, lo] = coef[...]
    for y in range(2):
        first[2 : 2 + count, y] = left[y * count : (y + 1) * count]
        first[2 : 2 + count, 2 + rows + y] = right[y * count : (y + 1) * count]
    weights[1 : 1 + count, 1 : 1 + rows] = weight[...]
    weights[1 : 1 + count, 0] = left[2 * count, :count]
    weights[1 : 1 + count, 1 + rows] = right[2 * count, :count]
    weights[0, 1 : 1 + rows] = down[2 * rows + 2]
    weights[1 + count, 1 : 1 + rows] = up[2 * rows + 2]

    def update(field, i, ys, size, before, wrow):
        cells = field[i, ys : ys + size]
        after = slope(field[i + 1, ys : ys + size] - cells)
        sides = slope(field[i, ys : ys + size + 1] - field[i, ys - 1 : ys + size])
        total = (after - before) + (sides[1:] - sides[:-1]) + along_z(cells)
        return cells + step_size * wrow[:, None, :] * total, after

    before = slope(first[1, lo] - first[0, lo])
    for i in range(1, planes - 1):
        edge = i == 1 or i == planes - 2
        ys, size = (2, rows) if edge else (1, rows + 2)
        if i == 2:
            before = slope(first[2, hi] - first[1, hi])
        if i == planes - 2:
            before = before[1 : 1 + rows]
        fresh, before = update(first, i, ys, size, before, weights[i - 1, ys - 1 : ys - 1 + size])
        second[i - 1, ys - 1 : ys - 1 + size] = fresh
    before = slope(second[1, 1 : 1 + rows] - second[0, 1 : 1 + rows])
    for i in range(1, count + 1):
        fresh, before = update(second, i, 1, rows, before, weights[i, 1 : 1 + rows])
        for y in range(rows):
            out[:, i - 1, y] = fresh[y]


def smooth(coef, left, right, down, up, tv_weight):
    count, rows, rank, width = coef.shape
    vmem = pl.BlockSpec(memory_space=pltpu.VMEM)
    return pl.pallas_call(
        smooth_kernel,
        out_shape=jax.ShapeDtypeStruct((rank, count, rows, width), jnp.float32),
        in_specs=[vmem] * 6,
        out_specs=vmem,
        scratch_shapes=[
            pltpu.VMEM((count + 4, rows + 4, rank, width), jnp.float32),
            pltpu.VMEM((count + 2, rows + 2, rank, width), jnp.float32),
            pltpu.VMEM((count + 2, rows + 2, width), jnp.float32),
        ],
        compiler_params=pltpu.CompilerParams(vmem_limit_bytes=limit),
        name="smooth",
    )(coef, left, right, down, up, tv_weight)


def neighbours(axis, toward_low, toward_high):
    ends = lax.axis_size(axis) - 1
    return (
        lax.ppermute(toward_high, axis, [(i, i + 1) for i in range(ends)]),
        lax.ppermute(toward_low, axis, [(i + 1, i) for i in range(ends)]),
    )


def on_device(signals, tile_flags, basis_old, tv_weight):
    frames, size_x, size_y, size_z = signals.shape
    rank = basis_old.shape[1]
    select = jnp.asarray(np.repeat(np.eye(frames), size_y, axis=1), jnp.bfloat16)
    parts = local_grown(signals, tile_flags, basis_old, select, lax.axis_size("grp"))
    parts = lax.all_to_all(parts, "grp", 0, 0)
    parts = sum_and_copy(parts, lax.axis_size("dev"))
    parts = lax.all_to_all(parts, "dev", 0, 0)
    basis, coef, head, tail = project(parts, signals, tile_flags, select, tv_weight, rank)
    left, right = neighbours("dev", head, tail)

    def face(far, near):
        return jnp.concatenate(
            [
                coef[far],
                left[size_x + near][None],
                coef[near],
                right[near][None],
                tv_weight[near][None],
            ],
            axis=0,
        )

    down, up = neighbours("grp", face(1, 0), face(size_x - 2, size_x - 1))
    return (basis.T, smooth(coef, left, right, down, up, tv_weight))


def solution(mesh):
    placed = (P(None, "grp", "dev", None), P("grp", "dev", None), P(), P("grp", "dev", None))
    return jax.shard_map(
        on_device,
        mesh=mesh,
        in_specs=placed,
        out_specs=(P(), P(None, "grp", "dev", None)),
        check_vma=False,
    )
```

time: 531 us -> 84.7 us (0.16)
  the two profiles are of different devices: /device:TPU:1 before, /device:TPU:39 now
where the time goes in v1:
time: 84.7 us; the launch traced here: 84.2 us
  blocking collectives  42.7 us (50%)
  Pallas kernels  13.5 us (16%)
  starting transfers between devices  10.7 us (13%)
  waiting for transfers between devices  9.13 us (11%)
  local copies, waits for them, and re-layouts  7.38 us (9%)
    all_to_all x1, blocking collectives, on_device(): parts = lax.all_to_all(parts, 'grp', 0, 0)  26 us
    all_to_all x1, blocking collectives, on_device(): parts = lax.all_to_all(parts, 'dev', 0, 0)  16.7 us
    unnamed x16, local copies, waits for them, and re-layouts  7.38 us
    ppermute x2, waiting for transfers between devices, neighbours(): lax.ppermute(toward_low, axis, [(i + 1, i) for i in range(ends)])  6.82 us
    ppermute x2, starting transfers between devices, neighbours(): lax.ppermute(toward_high, axis, [(i, i + 1) for i in range(ends)])  6.47 us
    pallas_call x1, Pallas kernels, local_grown(): pl.pallas_call(grown_kernel, out_shape=jax.ShapeDtypeStruct((copies, 3, 4...  5.77 us
    ppermute x2, starting transfers between devices, neighbours(): lax.ppermute(toward_low, axis, [(i + 1, i) for i in range(ends)])  4.2 us
    pallas_call x1, Pallas kernels, project(): pl.pallas_call(project_kernel, out_shape=(jax.ShapeDtypeStruct((rank, fra...  3.95 us
  transfers between devices with their start and end apart: 4, of which 3 were waited for; matrix products, arithmetic and copies ran while one was open for 0% of the time, Pallas kernels for 0%

profile of v1, /device:TPU:39, one launch (start us, length us, event | category | flops | bytes accessed | tf_op | source)
XLA Modules:
  0.0 84.2 jit_solution(12990945582647656348)
XLA Ops:
  0.6 0.0 copy-start.4
  0.6 0.8 copy.7.flags
  1.4 0.8 copy.8.basis_old
  2.3 0.0 copy-start
  2.3 2.3 %copy-done = bf16[192,6,8,256]{3,2,1,0:T(8,128)(2,1)S(1)} copy-done((bf16[192,6,8,256]{3,2,1,0:T(8,128)(2,1)S(1)}, bf16[192,6,8,256]{3,2,1,0:T(8,128)(2,1)}, u32[]{:S(2)}) %copy-start) | copy-done | bytes 4718616
  4.6 0.0 copy-start.2
  4.6 1.1 %copy-done.2 = bf16[192,1536]{1,0:T(8,128)(2,1)S(1)} copy-done((bf16[192,1536]{1,0:T(8,128)(2,1)S(1)}, bf16[192,1536]{1,0:T(8,128)(2,1)}, u32[]{:S(2)}) %copy-start.2) | copy-done | bytes 589848
  5.7 5.8 %local_grown.1 = f32[16,3,4,128]{3,2,1,0:T(4,128)S(1)} custom-call(bf16[192,6,8,256]{3,2,1,0:T(8,128)(2,1)S(1)} %copy-done, s32[6,8,2]{2,1,0:T(8,128)S(1)} %copy.7.flags, f32[192,8]{1,0:T(8,128)S(1)} %copy.8.basis_old, bf16[192,1536]{1,0:T(8,128)(2,1)S(1)} %copy-done.2), custom_call_target="tpu_custom_call" | custom-call | tf_op jit(solution)/shard_map/local_grown/pallas_call | solution.py:94
  11.4 26.0 %all_to_all.10.parts = f32[16,3,4,128]{3,2,1,0:T(4,128)} all-to-all(f32[16,3,4,128]{3,2,1,0:T(4,128)S(1)} %local_grown.1), channel_id=1, replica_groups=mesh['grp'=16,'dev'=32] {'grp'}, dimensions={0} | all-to-all | bytes 196608 | tf_op jit(solution)/shard_map/all_to_all | solution.py:269
  37.4 1.6 %sum_and_copy.1 = f32[32,3,4,128]{3,2,1,0:T(4,128)} custom-call(f32[16,3,4,128]{3,2,1,0:T(4,128)} %all_to_all.10.parts), custom_call_target="tpu_custom_call" | custom-call | tf_op jit(solution)/shard_map/sum_and_copy/pallas_call | solution.py:113
  39.0 16.7 %all_to_all.11.parts = f32[32,3,4,128]{3,2,1,0:T(4,128)S(1)} all-to-all(f32[32,3,4,128]{3,2,1,0:T(4,128)} %sum_and_copy.1), channel_id=1, replica_groups=mesh['grp'=16,'dev'=32] {'dev'}, dimensions={0} | all-to-all | bytes 393216 | tf_op jit(solution)/shard_map/all_to_all | solution.py:271
  55.8 0.0 copy-done.4
  55.8 0.0 copy-done.3
  55.8 2.3 %copy-done.1 = bf16[192,6,8,256]{3,2,1,0:T(8,128)(2,1)S(1)} copy-done((bf16[192,6,8,256]{3,2,1,0:T(8,128)(2,1)S(1)}, bf16[192,6,8,256]{3,2,1,0:T(8,128)(2,1)}, u32[]{:S(2)}) %copy-start.1) | copy-done | bytes 4718616
  58.1 4.0 %project.1 = (f32[8,192]{1,0:T(8,128)}, f32[6,8,8,256]{3,2,1,0:T(8,128)S(1)}, f32[13,8,256]{2,1,0:T(8,128)S(1)}, f32[13,8,256]{2,1,0:T(8,128)S(1)}) custom-call(f32[32,3,4,128]{3,2,1,0:T(4,128)S(1)} %all_to_all.11.parts, bf16[192,6,8,256]{3,2,1,0:T(8,128)(2,1)S(1)} %copy-done.1, s32[6,8,2]{2,1,0:T(8,128)S(1)} %copy.7.flags, bf16[192,1536]{1,0:T(8,128)(2,1)S(1)} %copy-done.3, ...), custom_call_target="tpu_custom_call" | custom-call | tf_op jit(solution)/shard_map/project/pallas_call | solution.py:164
  62.1 3.5 %collective-permute-start = (f32[13,8,256]{2,1,0:T(8,128)S(1)}, f32[13,8,256]{2,1,0:T(8,128)S(1)}, u32[]{:S(2)}, u32[]{:S(2)}) collective-permute-start(f32[13,8,256]{2,1,0:T(8,128)S(1)} %get-tuple-element.8), channel_id=1, source_target_pairs={{0,1},{1,2},{2,3},{3,4},{4,5},{5,6},{6,7},{7,8},{8,9},{9,10},{10,1... | collective-permute-start | bytes 319496 | tf_op jit(solution)/shard_map/ppermute | solution.py:259
  65.6 1.9 %collective-permute-start.1 = (f32[13,8,256]{2,1,0:T(8,128)S(1)}, f32[13,8,256]{2,1,0:T(8,128)S(1)}, u32[]{:S(2)}, u32[]{:S(2)}) collective-permute-start(f32[13,8,256]{2,1,0:T(8,128)S(1)} %get-tuple-element.9), channel_id=1, source_target_pairs={{1,0},{2,1},{3,2},{4,3},{5,4},{6,5},{7,6},{8,7},{9,8},{10,9},{11,1... | collective-permute-start | bytes 319496 | tf_op jit(solution)/shard_map/ppermute | solution.py:260
  67.5 0.0 collective-permute-done.left
  67.6 6.1 %collective-permute-done.1.right = f32[13,8,256]{2,1,0:T(8,128)S(1)} collective-permute-done((f32[13,8,256]{2,1,0:T(8,128)S(1)}, f32[13,8,256]{2,1,0:T(8,128)S(1)}, u32[]{:S(2)}, u32[]{:S(2)}) %collective-permute-start.1) | collective-permute-done | bytes 106528 | tf_op jit(solution)/shard_map/ppermute | solution.py:260
  73.7 2.3 %collective-permute-start.3 = (f32[19,8,256]{2,1,0:T(8,128)S(1)}, f32[19,8,256]{2,1,0:T(8,128)S(1)}, u32[]{:S(2)}, u32[]{:S(2)}) collective-permute-start(f32[19,8,256]{2,1,0:T(8,128)S(1)} %get-tuple-element.18), channel_id=1, source_target_pairs={{32,0},{64,32},{96,64},{128,96},{160,128},{192,160},{224,192},{256... | collective-permute-start | bytes 466952 | tf_op jit(solution)/shard_map/ppermute | solution.py:260
  76.0 3.0 %collective-permute-start.2 = (f32[19,8,256]{2,1,0:T(8,128)S(1)}, f32[19,8,256]{2,1,0:T(8,128)S(1)}, u32[]{:S(2)}, u32[]{:S(2)}) collective-permute-start(f32[19,8,256]{2,1,0:T(8,128)S(1)} %get-tuple-element.19), channel_id=1, source_target_pairs={{0,32},{32,64},{64,96},{96,128},{128,160},{160,192},{192,224},{224... | collective-permute-start | bytes 466952 | tf_op jit(solution)/shard_map/ppermute | solution.py:259
  79.0 0.7 collective-permute-done.3.up
  79.7 2.3 %collective-permute-done.2.down = f32[19,8,256]{2,1,0:T(8,128)S(1)} collective-permute-done((f32[19,8,256]{2,1,0:T(8,128)S(1)}, f32[19,8,256]{2,1,0:T(8,128)S(1)}, u32[]{:S(2)}, u32[]{:S(2)}) %collective-permute-start.2) | collective-permute-done | bytes 155680 | tf_op jit(solution)/shard_map/ppermute | solution.py:259
  82.0 2.2 %smooth.1 = f32[8,6,8,256]{3,2,1,0:T(8,128)} custom-call(f32[6,8,8,256]{3,2,1,0:T(8,128)S(1)} %get-tuple-element.7.coef, f32[13,8,256]{2,1,0:T(8,128)S(1)} %collective-permute-done.left, f32[13,8,256]{2,1,0:T(8,128)S(1)} %collective-permute-done.1.right, f32[19,8,256]{2,1,0:T(8,128)S(1)} %collective-permute-done.2.down, ...), custom_call_target="tpu_custom_call" | custom-call | tf_op jit(solution)/shard_map/smooth/pallas_call | solution.py:241
  (7 shorter events, 0.0 us)
Async XLA Ops:
  0.6 55.2 %copy-start.4 = (f32[6,8,256]{2,1,0:T(8,128)S(1)}, f32[6,8,256]{2,1,0:T(8,128)}, u32[]{:S(2)}) copy-start(f32[6,8,256]{2,1,0:T(8,128)} %weight.3) | copy-start | bytes 147460
  2.3 2.3 %copy-start = (bf16[192,6,8,256]{3,2,1,0:T(8,128)(2,1)S(1)}, bf16[192,6,8,256]{3,2,1,0:T(8,128)(2,1)}, u32[]{:S(2)}) copy-start(bf16[192,6,8,256]{3,2,1,0:T(8,128)(2,1)} %signals.3) | copy-start | bytes 14155780
  4.6 1.1 %copy-start.2 = (bf16[192,1536]{1,0:T(8,128)(2,1)S(1)}, bf16[192,1536]{1,0:T(8,128)(2,1)}, u32[]{:S(2)}) copy-start(bf16[192,1536]{1,0:T(8,128)(2,1)} %constant.2.clone.select) | copy-start | bytes 1769476
  5.7 50.1 %copy-start.3 = (bf16[192,1536]{1,0:T(8,128)(2,1)S(1)}, bf16[192,1536]{1,0:T(8,128)(2,1)}, u32[]{:S(2)}) copy-start(bf16[192,1536]{1,0:T(8,128)(2,1)} %constant.2.clone.select) | copy-start | bytes 1769476
  55.8 2.3 %copy-start.1 = (bf16[192,6,8,256]{3,2,1,0:T(8,128)(2,1)S(1)}, bf16[192,6,8,256]{3,2,1,0:T(8,128)(2,1)}, u32[]{:S(2)}) copy-start(bf16[192,6,8,256]{3,2,1,0:T(8,128)(2,1)} %signals.3) | copy-start | bytes 14155780
  62.1 5.4 %collective-permute-start = (f32[13,8,256]{2,1,0:T(8,128)S(1)}, f32[13,8,256]{2,1,0:T(8,128)S(1)}, u32[]{:S(2)}, u32[]{:S(2)}) collective-permute-start(f32[13,8,256]{2,1,0:T(8,128)S(1)} %get-tuple-element.8), channel_id=1, source_target_pairs={{0,1},{1,2},{2,3},{3,4},{4,5},{5,6},{6,7},{7,8},{8,9},{9,10},{10,1... | collective-permute-start | bytes 319496 | tf_op jit(solution)/shard_map/ppermute | solution.py:259
  65.6 8.1 %collective-permute-start.1 = (f32[13,8,256]{2,1,0:T(8,128)S(1)}, f32[13,8,256]{2,1,0:T(8,128)S(1)}, u32[]{:S(2)}, u32[]{:S(2)}) collective-permute-start(f32[13,8,256]{2,1,0:T(8,128)S(1)} %get-tuple-element.9), channel_id=1, source_target_pairs={{1,0},{2,1},{3,2},{4,3},{5,4},{6,5},{7,6},{8,7},{9,8},{10,9},{11,1... | collective-permute-start | bytes 319496 | tf_op jit(solution)/shard_map/ppermute | solution.py:260
  73.7 6.0 %collective-permute-start.3 = (f32[19,8,256]{2,1,0:T(8,128)S(1)}, f32[19,8,256]{2,1,0:T(8,128)S(1)}, u32[]{:S(2)}, u32[]{:S(2)}) collective-permute-start(f32[19,8,256]{2,1,0:T(8,128)S(1)} %get-tuple-element.18), channel_id=1, source_target_pairs={{32,0},{64,32},{96,64},{128,96},{160,128},{192,160},{224,192},{256... | collective-permute-start | bytes 466952 | tf_op jit(solution)/shard_map/ppermute | solution.py:260
  76.0 6.0 %collective-permute-start.2 = (f32[19,8,256]{2,1,0:T(8,128)S(1)}, f32[19,8,256]{2,1,0:T(8,128)S(1)}, u32[]{:S(2)}, u32[]{:S(2)}) collective-permute-start(f32[19,8,256]{2,1,0:T(8,128)S(1)} %get-tuple-element.19), channel_id=1, source_target_pairs={{0,32},{32,64},{64,96},{96,128},{128,160},{160,192},{192,224},{224... | collective-permute-start | bytes 466952 | tf_op jit(solution)/shard_map/ppermute | solution.py:259

commit v2 on v1

v2 whole, which is shorter than its diff:
```python
import jax
import jax.numpy as jnp
from jax import lax
from jax.experimental import pallas as pl
from jax.experimental.pallas import tpu as pltpu
from jax.sharding import PartitionSpec as P

step_size = 0.08
limit = 44 * 1024 * 1024
ahead = 3
held = 3
NT = (((1,), (1,)), ((), ()))
TN = (((0,), (0,)), ((), ()))


def dot(a, b, dims=(((1,), (0,)), ((), ()))):
    return lax.dot_general(a, b, dims, preferred_element_type=jnp.float32)


def terms(values, count):
    parts = []
    for _ in range(count):
        part = values.astype(jnp.bfloat16)
        parts.append(part)
        values = values - part.astype(jnp.float32)
    return parts


def spread_rows(repeated, rows):
    lane = lax.broadcasted_iota(jnp.int32, repeated.shape, 1) % rows
    return [jnp.where(lane == y, repeated, 0.0) for y in range(rows)]


def to_dense(values):
    rest = values[:, 128:]
    tail = jnp.concatenate([rest[:4], rest[4:]], axis=1)
    return jnp.stack([values[:4, :128], values[4:, :128], tail])


def from_dense(values):
    first = jnp.concatenate([values[0], values[1]], axis=0)
    rest = jnp.concatenate([values[2, :, :64], values[2, :, 64:]], axis=0)
    return jnp.concatenate([first, rest], axis=1)


def frame_select(frames, rows):
    shape = (frames, frames * rows)
    lane = lax.broadcasted_iota(jnp.int32, shape, 1) // rows
    return (lane == lax.broadcasted_iota(jnp.int32, shape, 0)).astype(jnp.bfloat16)


def tile_masks(flags, width):
    tiles = flags.shape[1]
    shape = (tiles, width)
    lane = lax.broadcasted_iota(jnp.int32, shape, 1) // (width // tiles)
    spread = (lane == lax.broadcasted_iota(jnp.int32, shape, 0)).astype(jnp.bfloat16)
    return [dot(flags[x].astype(jnp.bfloat16), spread, TN)[:, None, :] for x in range(flags.shape[0])]


def plane_refs(kept, spare):
    return [kept.at[i] for i in range(kept.shape[0])] + [spare.at[i] for i in range(spare.shape[0])]


def rows_of(plane):
    frames, rows, width = plane.shape
    return plane.reshape(frames * rows, width)


def mixing(rows_by_frame, select, count, rows):
    spread = []
    for part in terms(rows_by_frame, count):
        spread += spread_rows(dot(part, select), rows)
    return jnp.concatenate(spread, axis=0).astype(jnp.bfloat16)


def grown_kernel(signals, flags_in, basis_in, out, kept, spare, flags, basis_old, sems, small):
    first = [
        pltpu.make_async_copy(basis_in, basis_old, small.at[0]),
        pltpu.make_async_copy(flags_in, flags, small.at[1]),
    ]
    for copy in first:
        copy.start()
    frames, count, rows, width = signals.shape
    planes = plane_refs(kept, spare)
    copies = [pltpu.make_async_copy(signals.at[:, i], planes[i], sems.at[i]) for i in range(count)]
    for i in range(ahead):
        copies[i].start(priority=i % 2)
    rank = basis_old.shape[0]
    select = frame_select(frames, rows)
    for copy in first:
        copy.wait()
    weights = mixing(basis_old[...], select, 3, rows)
    keep = tile_masks(flags, width)

    def mix(i):
        copies[i].wait()
        if i + ahead < count:
            copies[i + ahead].start(priority=(i + ahead) % 2)
        flat = rows_of(planes[i][...])
        mixed = dot(weights, flat).reshape(3, rows, rank, width).sum(0) * keep[i]
        return jnp.concatenate(terms(mixed.reshape(rows * rank, width), 3), axis=0), flat

    def product(mixed, flat):
        return dot(mixed, flat, NT).reshape(3, rows, rank, frames * rows).sum(0)

    before = mix(0)
    total = jnp.zeros((rows, rank, frames * rows), jnp.float32)
    for i in range(1, count):
        now = mix(i)
        total = total + product(*before)
        before = now
    total = total + product(*before)
    lane = lax.broadcasted_iota(jnp.int32, (rank, frames * rows), 1) % rows
    diagonal = jnp.zeros((rank, frames * rows), jnp.float32)
    for y in range(rows):
        diagonal = diagonal + jnp.where(lane == y, total[y], 0.0)
    grown = dot(jnp.concatenate(terms(diagonal, 3), axis=0), select, NT)
    grown = grown.reshape(3, rank, frames).sum(0)
    out[...] = jnp.broadcast_to(to_dense(grown)[None], out.shape)


def local_grown(signals, flags, basis_old, copies):
    frames, size_x, size_y, size_z = signals.shape
    return pl.pallas_call(
        grown_kernel,
        out_shape=(
            jax.ShapeDtypeStruct((copies, 3, 4, 128), jnp.float32),
            jax.ShapeDtypeStruct((held, frames, size_y, size_z), signals.dtype),
        ),
        in_specs=[pl.BlockSpec(memory_space=pltpu.HBM)] * 3,
        out_specs=[pl.BlockSpec(memory_space=pltpu.VMEM)] * 2,
        scratch_shapes=[
            pltpu.VMEM((size_x - held, frames, size_y, size_z), signals.dtype),
            pltpu.VMEM(flags.shape, flags.dtype),
            pltpu.VMEM(basis_old.shape, basis_old.dtype),
            pltpu.SemaphoreType.DMA((size_x,)),
            pltpu.SemaphoreType.DMA((2,)),
        ],
        compiler_params=pltpu.CompilerParams(vmem_limit_bytes=limit),
        name="local_grown",
    )(signals, flags, basis_old)


def orthonormal(grown):
    rank = grown.shape[0]
    row = lax.broadcasted_iota(jnp.int32, (rank, 1), 0)
    for k in range(rank):
        pivot = grown[k : k + 1]
        inner = jnp.sum(grown * pivot, axis=1, keepdims=True)
        norm2 = inner[k : k + 1]
        scaled = pivot * (1.0 / norm2)
        grown = jnp.where(row > k, grown - inner * scaled, grown)
        grown = jnp.where(row == k, pivot / jnp.sqrt(norm2), grown)
    return grown


def project_kernel(parts, kept, signals, flags, weight, basis_out, coef, chip, gap, side, spare, sems):
    frames, count, rows, width = signals.shape
    planes = plane_refs(kept, spare)
    copies = [pltpu.make_async_copy(signals.at[:, i], planes[i], sems.at[i - held]) for i in range(held, count)]
    for copy in copies:
        copy.start()
    even = (lax.axis_index("dev") & 1) == 0
    side[...] = jnp.broadcast_to(jnp.where(even, 1, 0), side.shape)
    select = frame_select(frames, rows)
    keep = tile_masks(flags, width)
    basis = orthonormal(from_dense(jnp.sum(parts[...], axis=0)))
    rank = basis.shape[0]
    basis_out[...] = basis
    weights = mixing(basis, select, 2, rows)
    for i in range(count):
        if i >= held:
            copies[i - held].wait()
        mixed = dot(weights, rows_of(planes[i][...])).reshape(2, rows, rank, width).sum(0) * keep[i]
        coef[i] = mixed
        for y in range(2):
            chip[y * count + i] = jnp.where(even, mixed[rows - 2 + y], mixed[y])
            gap[y * count + i] = jnp.where(even, mixed[y], mixed[rows - 2 + y])
    blank = jnp.zeros((rank - count, width), jnp.float32)
    chip[2 * count, :count] = jnp.where(even, weight[:, rows - 1], weight[:, 0])
    gap[2 * count, :count] = jnp.where(even, weight[:, 0], weight[:, rows - 1])
    chip[2 * count, count:] = blank
    gap[2 * count, count:] = blank


def project(parts, kept, signals, flags, tv_weight, rank):
    frames, size_x, size_y, size_z = signals.shape
    edge = jax.ShapeDtypeStruct((2 * size_x + 1, rank, size_z), jnp.float32)
    vmem = pl.BlockSpec(memory_space=pltpu.VMEM)
    return pl.pallas_call(
        project_kernel,
        out_shape=(
            jax.ShapeDtypeStruct((rank, frames), jnp.float32),
            jax.ShapeDtypeStruct((size_x, size_y, rank, size_z), jnp.float32),
            edge,
            edge,
            jax.ShapeDtypeStruct((rank, size_z), jnp.int32),
        ),
        in_specs=[vmem, vmem, pl.BlockSpec(memory_space=pltpu.HBM), vmem, vmem],
        out_specs=(vmem,) * 5,
        scratch_shapes=[
            pltpu.VMEM((size_x - held, frames, size_y, size_z), signals.dtype),
            pltpu.SemaphoreType.DMA((size_x - held,)),
        ],
        compiler_params=pltpu.CompilerParams(vmem_limit_bytes=limit),
        name="project",
    )(parts, kept, signals, flags, tv_weight)


def slope(diff):
    return diff * lax.rsqrt(1.0 + diff * diff)


def along_z(cells):
    width = cells.shape[-1]
    lane = lax.broadcasted_iota(jnp.int32, cells.shape, cells.ndim - 1)
    above = jnp.where(lane == width - 1, 0.0, pltpu.roll(cells, width - 1, cells.ndim - 1))
    flux = slope(above - cells)
    below = jnp.where(lane == 0, slope(cells), pltpu.roll(flux, 1, cells.ndim - 1))
    return flux - below


def smooth_kernel(coef, left, right, down, up, weight, out, first, second, weights):
    count, rows, rank, width = coef.shape
    planes = count + 4
    lo, hi = slice(2, 2 + rows), slice(1, 3 + rows)
    for side, far, near in ((down, 0, 1), (up, planes - 1, planes - 2)):
        first[far, lo] = side[:rows]
        first[near, hi] = side[rows : 2 * rows + 2]
    first[2 : 2 + count, lo] = coef[...]
    for y in range(2):
        first[2 : 2 + count, y] = left[y * count : (y + 1) * count]
        first[2 : 2 + count, 2 + rows + y] = right[y * count : (y + 1) * count]
    weights[1 : 1 + count, 1 : 1 + rows] = weight[...]
    weights[1 : 1 + count, 0] = left[2 * count, :count]
    weights[1 : 1 + count, 1 + rows] = right[2 * count, :count]
    weights[0, 1 : 1 + rows] = down[2 * rows + 2]
    weights[1 + count, 1 : 1 + rows] = up[2 * rows + 2]

    def update(field, i, ys, size, before, wrow):
        cells = field[i, ys : ys + size]
        after = slope(field[i + 1, ys : ys + size] - cells)
        sides = slope(field[i, ys : ys + size + 1] - field[i, ys - 1 : ys + size])
        total = (after - before) + (sides[1:] - sides[:-1]) + along_z(cells)
        return cells + step_size * wrow[:, None, :] * total, after

    before = slope(first[1, lo] - first[0, lo])
    for i in range(1, planes - 1):
        edge = i == 1 or i == planes - 2
        ys, size = (2, rows) if edge else (1, rows + 2)
        if i == 2:
            before = slope(first[2, hi] - first[1, hi])
        if i == planes - 2:
            before = before[1 : 1 + rows]
        fresh, before = update(first, i, ys, size, before, weights[i - 1, ys - 1 : ys - 1 + size])
        second[i - 1, ys - 1 : ys - 1 + size] = fresh
    before = slope(second[1, 1 : 1 + rows] - second[0, 1 : 1 + rows])
    for i in range(1, count + 1):
        fresh, before = update(second, i, 1, rows, before, weights[i, 1 : 1 + rows])
        for y in range(rows):
            out[:, i - 1, y] = fresh[y]


def smooth(coef, left, right, down, up, tv_weight):
    count, rows, rank, width = coef.shape
    vmem = pl.BlockSpec(memory_space=pltpu.VMEM)
    return pl.pallas_call(
        smooth_kernel,
        out_shape=jax.ShapeDtypeStruct((rank, count, rows, width), jnp.float32),
        in_specs=[vmem] * 6,
        out_specs=vmem,
        scratch_shapes=[
            pltpu.VMEM((count + 4, rows + 4, rank, width), jnp.float32),
            pltpu.VMEM((count + 2, rows + 2, rank, width), jnp.float32),
            pltpu.VMEM((count + 2, rows + 2, width), jnp.float32),
        ],
        compiler_params=pltpu.CompilerParams(vmem_limit_bytes=limit),
        name="smooth",
    )(coef, left, right, down, up, tv_weight)


def neighbours(axis, toward_low, toward_high):
    ends = lax.axis_size(axis) - 1
    return (
        lax.ppermute(toward_high, axis, [(i, i + 1) for i in range(ends)]),
        lax.ppermute(toward_low, axis, [(i + 1, i) for i in range(ends)]),
    )


def neighbours_in_pairs(axis, gap, chip):
    count = lax.axis_size(axis)
    between = [(i, i + 1) for i in range(1, count - 1, 2)]
    return (
        lax.ppermute(gap, axis, between + [(j, i) for i, j in between]),
        lax.ppermute(chip, axis, [(i, i ^ 1) for i in range(count)]),
    )


def on_device(signals, tile_flags, basis_old, tv_weight):
    frames, size_x, size_y, size_z = signals.shape
    rank = basis_old.shape[1]
    flags = jnp.transpose(tile_flags, (0, 2, 1))
    pinned = [pltpu.with_memory_space_constraint(a, pltpu.HBM) for a in (signals, flags, basis_old.T)]
    parts, kept = local_grown(*pinned, lax.axis_size("grp"))
    parts = lax.all_to_all(parts, "grp", 0, 0)
    summed = jnp.sum(parts, axis=0)
    parts = jnp.broadcast_to(summed[None], (lax.axis_size("dev"),) + summed.shape)
    parts = lax.all_to_all(parts, "dev", 0, 0)
    basis, coef, chip, gap, even = project(parts, kept, pinned[0], flags, tv_weight, rank)
    gap, chip = neighbours_in_pairs("dev", gap, chip)
    left = jnp.where(even != 0, gap, chip)
    right = jnp.where(even != 0, chip, gap)

    def face(far, near):
        return jnp.concatenate(
            [coef[far], left[size_x + near][None], coef[near], right[near][None], tv_weight[near][None]], axis=0
        )

    down, up = neighbours("grp", face(1, 0), face(size_x - 2, size_x - 1))
    return (basis.T, smooth(coef, left, right, down, up, tv_weight))


def solution(mesh):
    placed = (P(None, "grp", "dev", None), P("grp", "dev", None), P(), P("grp", "dev", None))
    return jax.shard_map(
        on_device,
        mesh=mesh,
        in_specs=placed,
        out_specs=(P(), P(None, "grp", "dev", None)),
        check_vma=False,
    )
```

time: 84.7 us -> 72.7 us (0.86)
  the two profiles are of different devices: /device:TPU:39 before, /device:TPU:1 now
where the time goes in v2:
time: 72.7 us; the launch traced here: 72.4 us
  blocking collectives  45.2 us (62%)
  Pallas kernels  11.5 us (16%)
  starting transfers between devices  9.48 us (13%)
  waiting for transfers between devices  5.35 us (7%)
  between operations  0.75 us (1%)
    all_to_all x1, blocking collectives, on_device(): parts = lax.all_to_all(parts, 'grp', 0, 0)  27.4 us
    all_to_all x1, blocking collectives, on_device(): parts = lax.all_to_all(parts, 'dev', 0, 0)  17.8 us
    pallas_call x1, Pallas kernels, local_grown(): pl.pallas_call(grown_kernel, out_shape=(jax.ShapeDtypeStruct((copies, 3,...  5.46 us
    ppermute x1, starting transfers between devices, neighbours(): lax.ppermute(toward_high, axis, [(i, i + 1) for i in range(ends)])  4 us
    pallas_call x1, Pallas kernels, project(): pl.pallas_call(project_kernel, out_shape=(jax.ShapeDtypeStruct((rank, fra...  3.79 us
    ppermute x1, waiting for transfers between devices, neighbours(): lax.ppermute(toward_low, axis, [(i + 1, i) for i in range(ends)])  2.56 us
    ppermute x1, starting transfers between devices, neighbours_in_pairs(): lax.ppermute(gap, axis, between + [(j, i) for i, j in between])  2.27 us
    pallas_call x1, Pallas kernels, smooth(): pl.pallas_call(smooth_kernel, out_shape=jax.ShapeDtypeStruct((rank, count...  2.25 us
  transfers between devices with their start and end apart: 4, of which 3 were waited for; matrix products, arithmetic and copies ran while one was open for 0% of the time, Pallas kernels for 0%

profile of v2, /device:TPU:1, one launch (start us, length us, event | category | flops | bytes accessed | tf_op | source)
XLA Modules:
  0.0 72.4 jit_solution(895866656116378781)
XLA Ops:
  0.6 0.0 copy-start.1
  0.6 0.0 copy-start
  0.7 5.5 %local_grown.1 = (f32[16,3,4,128]{3,2,1,0:T(4,128)S(1)}, bf16[3,192,8,256]{3,2,1,0:T(8,128)(2,1)S(1)}) custom-call(bf16[192,6,8,256]{3,2,1,0:T(8,128)(2,1)} %signals.3, s32[6,2,8]{2,1,0:T(2,128)} %bitcast.11, f32[8,192]{1,0:T(8,128)} %bitcast.13), custom_call_target="tpu_custom_call" | custom-call | tf_op jit(solution)/shard_map/local_grown/pallas_call | solution.py:124
  6.1 27.4 %all_to_all.10 = f32[16,3,4,128]{3,2,1,0:T(4,128)S(1)} all-to-all(f32[16,3,4,128]{3,2,1,0:T(4,128)S(1)} %get-tuple-element.9), channel_id=1, replica_groups=mesh['grp'=16,'dev'=32] {'grp'}, dimensions={0} | all-to-all | bytes 196608 | tf_op jit(solution)/shard_map/all_to_all | solution.py:305
  33.6 17.8 %all_to_all.11.parts = f32[32,3,4,128]{3,2,1,0:T(4,128)S(1)} all-to-all(f32[32,3,4,128]{3,2,1,0:T(4,128)S(1)} %broadcast_in_dim.11), channel_id=1, replica_groups=mesh['grp'=16,'dev'=32] {'dev'}, dimensions={0} | all-to-all | bytes 393216 | tf_op jit(solution)/shard_map/all_to_all | solution.py:308
  51.4 0.0 copy-done.1
  51.4 0.0 copy-done
  51.4 3.8 %project.1 = (f32[8,192]{1,0:T(8,128)}, f32[6,8,8,256]{3,2,1,0:T(8,128)S(1)}, f32[13,8,256]{2,1,0:T(8,128)S(1)}, f32[13,8,256]{2,1,0:T(8,128)S(1)}, s32[8,256]{1,0:T(8,128)S(1)}) custom-call(f32[32,3,4,128]{3,2,1,0:T(4,128)S(1)} %all_to_all.11.parts, bf16[3,192,8,256]{3,2,1,0:T(8,128)(2,1)S(1)} %get-tuple-element.10.kept, bf16[192,6,8,256]{3,2,1,0:T(8,128)(2,1)} %signals.3, ...), custom_call_target="tpu_custom_call" | custom-call | tf_op jit(solution)/shard_map/project/pallas_call | solution.py:190
  55.2 2.3 %collective-permute-start = (f32[13,8,256]{2,1,0:T(8,128)S(1)}, f32[13,8,256]{2,1,0:T(8,128)S(1)}, u32[]{:S(2)}, u32[]{:S(2)}) collective-permute-start(f32[13,8,256]{2,1,0:T(8,128)S(1)} %get-tuple-element.14), channel_id=1, source_target_pairs={{1,2},{3,4},{5,6},{7,8},{9,10},{11,12},{13,14},{15,16},{17,18},{19... | collective-permute-start | bytes 319496 | tf_op jit(solution)/shard_map/ppermute | solution.py:294
  57.5 1.9 %collective-permute-start.1 = (f32[13,8,256]{2,1,0:T(8,128)S(1)}, f32[13,8,256]{2,1,0:T(8,128)S(1)}, u32[]{:S(2)}, u32[]{:S(2)}) collective-permute-start(f32[13,8,256]{2,1,0:T(8,128)S(1)} %get-tuple-element.15), channel_id=1, source_target_pairs={{0,1},{1,0},{2,3},{3,2},{4,5},{5,4},{6,7},{7,6},{8,9},{9,8},{10,11... | collective-permute-start | bytes 319496 | tf_op jit(solution)/shard_map/ppermute | solution.py:295
  59.4 1.8 %collective-permute-done = f32[13,8,256]{2,1,0:T(8,128)S(1)} collective-permute-done((f32[13,8,256]{2,1,0:T(8,128)S(1)}, f32[13,8,256]{2,1,0:T(8,128)S(1)}, u32[]{:S(2)}, u32[]{:S(2)}) %collective-permute-start) | collective-permute-done | bytes 106528 | tf_op jit(solution)/shard_map/ppermute | solution.py:294
  61.2 0.0 collective-permute-done.1
  61.3 1.3 %collective-permute-start.3 = (f32[19,8,256]{2,1,0:T(8,128)S(1)}, f32[19,8,256]{2,1,0:T(8,128)S(1)}, u32[]{:S(2)}, u32[]{:S(2)}) collective-permute-start(f32[19,8,256]{2,1,0:T(8,128)S(1)} %get-tuple-element.26), channel_id=1, source_target_pairs={{32,0},{64,32},{96,64},{128,96},{160,128},{192,160},{224,192},{256... | collective-permute-start | bytes 466952 | tf_op jit(solution)/shard_map/ppermute | solution.py:286
  62.6 4.0 %collective-permute-start.2 = (f32[19,8,256]{2,1,0:T(8,128)S(1)}, f32[19,8,256]{2,1,0:T(8,128)S(1)}, u32[]{:S(2)}, u32[]{:S(2)}) collective-permute-start(f32[19,8,256]{2,1,0:T(8,128)S(1)} %get-tuple-element.27), channel_id=1, source_target_pairs={{0,32},{32,64},{64,96},{96,128},{128,160},{160,192},{192,224},{224... | collective-permute-start | bytes 466952 | tf_op jit(solution)/shard_map/ppermute | solution.py:285
  66.6 2.6 %collective-permute-done.3.up = f32[19,8,256]{2,1,0:T(8,128)S(1)} collective-permute-done((f32[19,8,256]{2,1,0:T(8,128)S(1)}, f32[19,8,256]{2,1,0:T(8,128)S(1)}, u32[]{:S(2)}, u32[]{:S(2)}) %collective-permute-start.3) | collective-permute-done | bytes 155680 | tf_op jit(solution)/shard_map/ppermute | solution.py:286
  69.2 1.0 %collective-permute-done.2.down = f32[19,8,256]{2,1,0:T(8,128)S(1)} collective-permute-done((f32[19,8,256]{2,1,0:T(8,128)S(1)}, f32[19,8,256]{2,1,0:T(8,128)S(1)}, u32[]{:S(2)}, u32[]{:S(2)}) %collective-permute-start.2) | collective-permute-done | bytes 155680 | tf_op jit(solution)/shard_map/ppermute | solution.py:285
  70.2 2.2 %smooth.1 = f32[8,6,8,256]{3,2,1,0:T(8,128)} custom-call(f32[6,8,8,256]{3,2,1,0:T(8,128)S(1)} %get-tuple-element.12.coef, f32[13,8,256]{2,1,0:T(8,128)S(1)} %get-tuple-element.21.left, f32[13,8,256]{2,1,0:T(8,128)S(1)} %get-tuple-element.20.right, f32[19,8,256]{2,1,0:T(8,128)S(1)} %collective-permute-done.2.down, ...), custom_call_target="tpu_custom_call" | custom-call | tf_op jit(solution)/shard_map/smooth/pallas_call | solution.py:267
  (9 shorter events, 0.1 us)
Async XLA Ops:
  0.6 50.8 %copy-start.1 = (s32[6,8,2]{1,2,0:T(2,128)S(1)}, s32[6,8,2]{1,2,0:T(2,128)}, u32[]{:S(2)}) copy-start(s32[6,8,2]{1,2,0:T(2,128)} %param.5) | copy-start | bytes 1156
  0.6 50.8 %copy-start = (f32[6,8,256]{2,1,0:T(8,128)S(1)}, f32[6,8,256]{2,1,0:T(8,128)}, u32[]{:S(2)}) copy-start(f32[6,8,256]{2,1,0:T(8,128)} %weight.3) | copy-start | bytes 147460
  55.2 6.0 %collective-permute-start = (f32[13,8,256]{2,1,0:T(8,128)S(1)}, f32[13,8,256]{2,1,0:T(8,128)S(1)}, u32[]{:S(2)}, u32[]{:S(2)}) collective-permute-start(f32[13,8,256]{2,1,0:T(8,128)S(1)} %get-tuple-element.14), channel_id=1, source_target_pairs={{1,2},{3,4},{5,6},{7,8},{9,10},{11,12},{13,14},{15,16},{17,18},{19... | collective-permute-start | bytes 319496 | tf_op jit(solution)/shard_map/ppermute | solution.py:294
  57.5 3.7 %collective-permute-start.1 = (f32[13,8,256]{2,1,0:T(8,128)S(1)}, f32[13,8,256]{2,1,0:T(8,128)S(1)}, u32[]{:S(2)}, u32[]{:S(2)}) collective-permute-start(f32[13,8,256]{2,1,0:T(8,128)S(1)} %get-tuple-element.15), channel_id=1, source_target_pairs={{0,1},{1,0},{2,3},{3,2},{4,5},{5,4},{6,7},{7,6},{8,9},{9,8},{10,11... | collective-permute-start | bytes 319496 | tf_op jit(solution)/shard_map/ppermute | solution.py:295
  61.3 7.9 %collective-permute-start.3 = (f32[19,8,256]{2,1,0:T(8,128)S(1)}, f32[19,8,256]{2,1,0:T(8,128)S(1)}, u32[]{:S(2)}, u32[]{:S(2)}) collective-permute-start(f32[19,8,256]{2,1,0:T(8,128)S(1)} %get-tuple-element.26), channel_id=1, source_target_pairs={{32,0},{64,32},{96,64},{128,96},{160,128},{192,160},{224,192},{256... | collective-permute-start | bytes 466952 | tf_op jit(solution)/shard_map/ppermute | solution.py:286
  62.6 7.6 %collective-permute-start.2 = (f32[19,8,256]{2,1,0:T(8,128)S(1)}, f32[19,8,256]{2,1,0:T(8,128)S(1)}, u32[]{:S(2)}, u32[]{:S(2)}) collective-permute-start(f32[19,8,256]{2,1,0:T(8,128)S(1)} %get-tuple-element.27), channel_id=1, source_target_pairs={{0,32},{32,64},{64,96},{96,128},{128,160},{160,192},{192,224},{224... | collective-permute-start | bytes 466952 | tf_op jit(solution)/shard_map/ppermute | solution.py:285

commit v3 on v2

v3 whole, which is shorter than its diff:
```python
import jax
import jax.numpy as jnp
from jax import lax
from jax.experimental import pallas as pl
from jax.experimental.pallas import tpu as pltpu
from jax.sharding import PartitionSpec as P

step_size = 0.08
limit = 44 * 1024 * 1024
ahead = 4
NT = (((1,), (1,)), ((), ()))
TN = (((0,), (0,)), ((), ()))


def dot(a, b, dims=(((1,), (0,)), ((), ()))):
    return lax.dot_general(a, b, dims, preferred_element_type=jnp.float32)


def terms(values, count):
    parts = []
    for _ in range(count):
        part = values.astype(jnp.bfloat16)
        parts.append(part)
        values = values - part.astype(jnp.float32)
    return parts


def spread_rows(repeated, rows):
    lane = lax.broadcasted_iota(jnp.int32, repeated.shape, 1) % rows
    return [jnp.where(lane == y, repeated, 0.0) for y in range(rows)]


def to_dense(values):
    rest = values[:, 128:]
    tail = jnp.concatenate([rest[:4], rest[4:]], axis=1)
    return jnp.stack([values[:4, :128], values[4:, :128], tail])


def from_dense(values):
    first = jnp.concatenate([values[0], values[1]], axis=0)
    rest = jnp.concatenate([values[2, :, :64], values[2, :, 64:]], axis=0)
    return jnp.concatenate([first, rest], axis=1)


def frame_select(frames, rows):
    shape = (frames, frames * rows)
    lane = lax.broadcasted_iota(jnp.int32, shape, 1) // rows
    return (lane == lax.broadcasted_iota(jnp.int32, shape, 0)).astype(jnp.bfloat16)


def tile_masks(flags, width):
    tiles = flags.shape[1]
    shape = (tiles, width)
    lane = lax.broadcasted_iota(jnp.int32, shape, 1) // (width // tiles)
    spread = (lane == lax.broadcasted_iota(jnp.int32, shape, 0)).astype(jnp.bfloat16)
    return [dot(flags[x].astype(jnp.bfloat16), spread, TN)[:, None, :] for x in range(flags.shape[0])]


def outer_planes(count):
    return [0, 1, count - 2, count - 1]


def inner_planes(count):
    return list(range(2, count - 2))


def rows_of(plane):
    frames, rows, width = plane.shape
    return plane.reshape(frames * rows, width)


def mixing(rows_by_frame, select, count, rows):
    spread = []
    for part in terms(rows_by_frame, count):
        spread += spread_rows(dot(part, select), rows)
    return jnp.concatenate(spread, axis=0).astype(jnp.bfloat16)


def grown_kernel(signals, flags_in, basis_in, out, kept, spare, flags, basis_old, sems, small):
    first = [
        pltpu.make_async_copy(basis_in, basis_old, small.at[0]),
        pltpu.make_async_copy(flags_in, flags, small.at[1]),
    ]
    for copy in first:
        copy.start()
    frames, count, rows, width = signals.shape
    order = outer_planes(count) + inner_planes(count)
    planes = [kept.at[i] for i in range(kept.shape[0])] + [spare.at[i] for i in range(spare.shape[0])]
    copies = [pltpu.make_async_copy(signals.at[:, x], planes[i], sems.at[i]) for i, x in enumerate(order)]
    for i in range(ahead):
        copies[i].start(priority=i % 2)
    rank = basis_old.shape[0]
    select = frame_select(frames, rows)
    for copy in first:
        copy.wait()
    weights = mixing(basis_old[...], select, 3, rows)
    keep = tile_masks(flags, width)

    def mix(i):
        flat = rows_of(planes[i][...])
        mixed = dot(weights, flat).reshape(3, rows, rank, width).sum(0) * keep[order[i]]
        return jnp.concatenate(terms(mixed.reshape(rows * rank, width), 3), axis=0), flat

    def product(mixed, flat):
        return dot(mixed, flat, NT).reshape(3, rows, rank, frames * rows).sum(0)

    total = jnp.zeros((rows, rank, frames * rows), jnp.float32)
    before = []
    for start in range(0, count, 2):
        group = range(start, start + 2)
        for i in group:
            copies[i].wait()
        for i in group:
            if i + ahead < count:
                copies[i + ahead].start(priority=(i + ahead) % 2)
        now = [mix(i) for i in group]
        for pair in before:
            total = total + product(*pair)
        before = now
    for pair in before:
        total = total + product(*pair)
    lane = lax.broadcasted_iota(jnp.int32, (rank, frames * rows), 1) % rows
    diagonal = jnp.zeros((rank, frames * rows), jnp.float32)
    for y in range(rows):
        diagonal = diagonal + jnp.where(lane == y, total[y], 0.0)
    grown = dot(jnp.concatenate(terms(diagonal, 3), axis=0), select, NT)
    grown = grown.reshape(3, rank, frames).sum(0)
    out[...] = jnp.broadcast_to(to_dense(grown)[None], out.shape)


def local_grown(signals, flags, basis_old, copies):
    frames, size_x, size_y, size_z = signals.shape
    return pl.pallas_call(
        grown_kernel,
        out_shape=(
            jax.ShapeDtypeStruct((copies, 3, 4, 128), jnp.float32),
            jax.ShapeDtypeStruct((len(outer_planes(size_x)), frames, size_y, size_z), signals.dtype),
        ),
        in_specs=[pl.BlockSpec(memory_space=pltpu.HBM)] * 3,
        out_specs=[pl.BlockSpec(memory_space=pltpu.VMEM)] * 2,
        scratch_shapes=[
            pltpu.VMEM((len(inner_planes(size_x)), frames, size_y, size_z), signals.dtype),
            pltpu.VMEM(flags.shape, flags.dtype),
            pltpu.VMEM(basis_old.shape, basis_old.dtype),
            pltpu.SemaphoreType.DMA((size_x,)),
            pltpu.SemaphoreType.DMA((2,)),
        ],
        compiler_params=pltpu.CompilerParams(vmem_limit_bytes=limit),
        name="local_grown",
    )(signals, flags, basis_old)


def orthonormal(grown):
    rank = grown.shape[0]
    row = lax.broadcasted_iota(jnp.int32, (rank, 1), 0)
    for k in range(rank):
        pivot = grown[k : k + 1]
        inner = jnp.sum(grown * pivot, axis=1, keepdims=True)
        norm2 = inner[k : k + 1]
        scaled = pivot * (1.0 / norm2)
        grown = jnp.where(row > k, grown - inner * scaled, grown)
        grown = jnp.where(row == k, pivot / jnp.sqrt(norm2), grown)
    return grown


def projected(mixer, plane, keep, rank):
    frames, rows, width = plane.shape
    return dot(mixer, rows_of(plane)).reshape(2, rows, rank, width).sum(0) * keep


def project_outer_kernel(parts, kept, flags, weight, basis_out, mixer_out, low, high, side):
    count, rows, width = weight.shape
    frames = kept.shape[1]
    even = (lax.axis_index("dev") & 1) == 0
    side[...] = jnp.broadcast_to(jnp.where(even, 1, 0), side.shape)
    select = frame_select(frames, rows)
    keep = tile_masks(flags, width)
    basis = orthonormal(from_dense(jnp.sum(parts[...], axis=0)))
    rank = basis.shape[0]
    basis_out[...] = basis
    mixer = mixing(basis, select, 2, rows)
    mixer_out[...] = mixer
    for i, x in enumerate(outer_planes(count)):
        face = low if i < 2 else high
        face[(i % 2) * rows : (i % 2 + 1) * rows] = projected(mixer, kept[i], keep[x], rank)
    low[2 * rows] = weight[0]
    high[2 * rows] = weight[count - 1]


def project_outer(parts, kept, flags, tv_weight, rank):
    size_x, size_y, size_z = tv_weight.shape
    frames = kept.shape[1]
    face = jax.ShapeDtypeStruct((2 * size_y + 1, rank, size_z), jnp.float32)
    vmem = pl.BlockSpec(memory_space=pltpu.VMEM)
    return pl.pallas_call(
        project_outer_kernel,
        out_shape=(
            jax.ShapeDtypeStruct((rank, frames), jnp.float32),
            jax.ShapeDtypeStruct((2 * size_y * rank, frames * size_y), jnp.bfloat16),
            face,
            face,
            jax.ShapeDtypeStruct((rank, size_z), jnp.int32),
        ),
        in_specs=[vmem] * 4,
        out_specs=(vmem,) * 5,
        compiler_params=pltpu.CompilerParams(vmem_limit_bytes=limit),
        name="project_outer",
    )(parts, kept, flags, tv_weight)


def project_inner_kernel(signals, mixer, flags, weight, low, high, inner, gap, planes, sems):
    frames, count, rows, width = signals.shape
    copies = [
        pltpu.make_async_copy(signals.at[:, x], planes.at[i], sems.at[i]) for i, x in enumerate(inner_planes(count))
    ]
    for copy in copies:
        copy.start()
    rank = low.shape[1]
    even = (lax.axis_index("dev") & 1) == 0
    keep = tile_masks(flags, width)

    def edges(x, head, tail):
        for y in range(2):
            gap[y * count + x] = jnp.where(even, head[y], tail[y])

    for i, x in enumerate(outer_planes(count)):
        face, first = (low if i < 2 else high), (i % 2) * rows
        edges(x, face[first : first + 2], face[first + rows - 2 : first + rows])
    blank = jnp.zeros((rank - count, width), jnp.float32)
    gap[2 * count, :count] = jnp.where(even, weight[:, 0], weight[:, rows - 1])
    gap[2 * count, count:] = blank
    for i, x in enumerate(inner_planes(count)):
        copies[i].wait()
        plane = projected(mixer[...], planes[i], keep[x], rank)
        inner[i] = plane
        edges(x, plane[:2], plane[rows - 2 :])


def project_inner(signals, mixer, flags, tv_weight, low, high):
    frames, size_x, size_y, size_z = signals.shape
    rank = low.shape[1]
    inner = len(inner_planes(size_x))
    edge = jax.ShapeDtypeStruct((2 * size_x + 1, rank, size_z), jnp.float32)
    vmem = pl.BlockSpec(memory_space=pltpu.VMEM)
    return pl.pallas_call(
        project_inner_kernel,
        out_shape=(jax.ShapeDtypeStruct((inner, size_y, rank, size_z), jnp.float32), edge),
        in_specs=[pl.BlockSpec(memory_space=pltpu.HBM)] + [vmem] * 5,
        out_specs=(vmem,) * 2,
        scratch_shapes=[
            pltpu.VMEM((inner, frames, size_y, size_z), signals.dtype),
            pltpu.SemaphoreType.DMA((inner,)),
        ],
        compiler_params=pltpu.CompilerParams(vmem_limit_bytes=limit),
        cost_estimate=pl.CostEstimate(flops=1500000000, bytes_accessed=6000000, transcendentals=0),
        name="project_inner",
    )(signals, mixer, flags, tv_weight, low, high)


def slope(diff):
    return diff * lax.rsqrt(1.0 + diff * diff)


def along_z(cells):
    width = cells.shape[-1]
    lane = lax.broadcasted_iota(jnp.int32, cells.shape, cells.ndim - 1)
    above = jnp.where(lane == width - 1, 0.0, pltpu.roll(cells, width - 1, cells.ndim - 1))
    flux = slope(above - cells)
    below = jnp.where(lane == 0, slope(cells), pltpu.roll(flux, 1, cells.ndim - 1))
    return flux - below


def update(planes, i, ys, size, before, weight):
    cells = planes[i][ys : ys + size]
    after = slope(planes[i + 1][ys : ys + size] - cells)
    sides = slope(planes[i][ys : ys + size + 1] - planes[i][ys - 1 : ys + size])
    total = (after - before) + (sides[1:] - sides[:-1]) + along_z(cells)
    return cells + step_size * weight[:, None, :] * total, after


def x_planes(low, inner, high, down, up):
    rows = inner.shape[1]
    faces = [[face.at[:rows], face.at[rows : 2 * rows]] for face in (down, low, high, up)]
    return faces[0] + faces[1] + [inner.at[i] for i in range(inner.shape[0])] + faces[2] + faces[3]


def smooth_middle_kernel(low, inner, high, down, up, weight, once, twice, chip):
    count, rows, width = weight.shape
    rank = low.shape[1]
    planes = x_planes(low, inner, high, down, up)
    even = (lax.axis_index("dev") & 1) == 0
    for x in range(count):
        for y in range(2):
            chip[y * count + x] = jnp.where(even, planes[x + 2][rows - 2 + y], planes[x + 2][y])
    chip[2 * count, :count] = jnp.where(even, weight[:, rows - 1], weight[:, 0])
    chip[2 * count, count:] = jnp.zeros((rank - count, width), jnp.float32)
    for i, plane in enumerate((planes[1], planes[count + 2])):
        chip[2 * count + 1 + i] = jnp.where(even, plane[rows - 1], plane[0])
    weights = [down.at[2 * rows]] + [weight.at[x] for x in range(count)] + [up.at[2 * rows]]
    size = rows - 2
    before = slope(planes[1][1 : 1 + size] - planes[0][1 : 1 + size])
    for i in range(1, count + 3):
        fresh, before = update(planes, i, 1, size, before, weights[i - 1][1 : 1 + size])
        once[i - 1] = fresh
    planes = [once.at[i] for i in range(count + 2)]
    size = rows - 4
    before = slope(planes[1][1 : 1 + size] - planes[0][1 : 1 + size])
    for i in range(1, count + 1):
        fresh, before = update(planes, i, 1, size, before, weight[i - 1, 2 : 2 + size])
        twice[i - 1] = fresh


def smooth_middle(low, inner, high, down, up, tv_weight):
    count, rows, width = tv_weight.shape
    rank = low.shape[1]
    vmem = pl.BlockSpec(memory_space=pltpu.VMEM)
    return pl.pallas_call(
        smooth_middle_kernel,
        out_shape=(
            jax.ShapeDtypeStruct((count + 2, rows - 2, rank, width), jnp.float32),
            jax.ShapeDtypeStruct((count, rows - 4, rank, width), jnp.float32),
            jax.ShapeDtypeStruct((2 * count + 3, rank, width), jnp.float32),
        ),
        in_specs=[vmem] * 6,
        out_specs=(vmem,) * 3,
        compiler_params=pltpu.CompilerParams(vmem_limit_bytes=limit),
        cost_estimate=pl.CostEstimate(flops=50000000, bytes_accessed=3000000, transcendentals=1000000),
        name="smooth_middle",
    )(low, inner, high, down, up, tv_weight)


def smooth_edges_kernel(low, inner, high, down, up, left, right, once, twice, weight, out, field, fresher):
    count, rows, width = weight.shape
    planes = x_planes(low, inner, high, down, up)
    last = len(planes) - 1
    for x in range(count):
        for y in range(2, rows - 2):
            out[:, x, y] = twice[x, y - 2]
    for side, received in enumerate((left, right)):
        edge = 1 if side else 2
        mine, theirs, shift = (0, 2, 2) if side else (2, 0, 0)
        outer = rows - 1 if side else 0
        own = slice(rows - 2, rows) if side else slice(0, 2)
        cells = [field.at[side, i] for i in range(last + 1)]
        for i in range(last + 1):
            cells[i][mine : mine + 2] = planes[i][own]
        for x in range(count):
            for y in range(2):
                cells[x + 2][theirs + y] = received[y * count + x]
        cells[1][3 - edge] = received[2 * count + 1]
        cells[last - 1][3 - edge] = received[2 * count + 2]
        before = slope(cells[1][edge : edge + 1] - cells[0][edge : edge + 1])
        fresh, _ = update(cells, 1, edge, 1, before, down[2 * rows, outer : outer + 1])
        fresher[side, 0, shift + edge - 1] = fresh[0]
        before = slope(cells[2][1:3] - cells[1][1:3])
        for x in range(count):
            pair = [weight[x, outer : outer + 1], received[2 * count, x : x + 1]]
            pair = jnp.concatenate(pair if side else pair[::-1], axis=0)
            fresh, before = update(cells, x + 2, 1, 2, before, pair)
            fresher[side, x + 1, shift : shift + 2] = fresh
        before = before[edge - 1 : edge]
        fresh, _ = update(cells, last - 1, edge, 1, before, up[2 * rows, outer : outer + 1])
        fresher[side, count + 1, shift + edge - 1] = fresh[0]
        done = slice(rows - 4, rows - 2) if side else slice(0, 2)
        cells = [fresher.at[side, i] for i in range(count + 2)]
        for i in range(count + 2):
            cells[i][2 - shift : 4 - shift] = once[i, done]
        before = slope(cells[1][1:3] - cells[0][1:3])
        for x in range(count):
            fresh, before = update(cells, x + 1, 1, 2, before, weight[x, own])
            for y in range(2):
                out[:, x, own.start + y] = fresh[y]


def smooth_edges(low, inner, high, down, up, left, right, once, twice, tv_weight):
    count, rows, width = tv_weight.shape
    rank = low.shape[1]
    vmem = pl.BlockSpec(memory_space=pltpu.VMEM)
    return pl.pallas_call(
        smooth_edges_kernel,
        out_shape=jax.ShapeDtypeStruct((rank, count, rows, width), jnp.float32),
        in_specs=[vmem] * 10,
        out_specs=vmem,
        scratch_shapes=[
            pltpu.VMEM((2, count + 4, 4, rank, width), jnp.float32),
            pltpu.VMEM((2, count + 2, 4, rank, width), jnp.float32),
        ],
        compiler_params=pltpu.CompilerParams(vmem_limit_bytes=limit),
        name="smooth_edges",
    )(low, inner, high, down, up, left, right, once, twice, tv_weight)


def neighbours(axis, toward_low, toward_high):
    ends = lax.axis_size(axis) - 1
    return (
        lax.ppermute(toward_high, axis, [(i, i + 1) for i in range(ends)]),
        lax.ppermute(toward_low, axis, [(i + 1, i) for i in range(ends)]),
    )


def neighbours_in_pairs(axis, gap, chip):
    count = lax.axis_size(axis)
    between = [(i, i + 1) for i in range(1, count - 1, 2)]
    return (
        lax.ppermute(gap, axis, between + [(j, i) for i, j in between]),
        lax.ppermute(chip, axis, [(i, i ^ 1) for i in range(count)]),
    )


def on_device(signals, tile_flags, basis_old, tv_weight):
    frames, size_x, size_y, size_z = signals.shape
    rank = basis_old.shape[1]
    flags = jnp.transpose(tile_flags, (0, 2, 1))
    pinned = [pltpu.with_memory_space_constraint(a, pltpu.HBM) for a in (signals, flags, basis_old.T)]
    parts, kept = local_grown(*pinned, lax.axis_size("grp"))
    parts = lax.all_to_all(parts, "grp", 0, 0)
    summed = jnp.sum(parts, axis=0)
    parts = jnp.broadcast_to(summed[None], (lax.axis_size("dev"),) + summed.shape)
    parts = lax.all_to_all(parts, "dev", 0, 0)
    basis, mixer, low, high, even = project_outer(parts, kept, flags, tv_weight, rank)
    down, up = neighbours("grp", low, high)
    inner, gap = project_inner(pinned[0], mixer, flags, tv_weight, low, high)
    heads = jnp.stack([down[size_y], up[0]])
    tails = jnp.stack([down[2 * size_y - 1], up[size_y - 1]])
    gap = jnp.concatenate([gap, jnp.where(even != 0, heads, tails)], axis=0)
    once, twice, chip = smooth_middle(low, inner, high, down, up, tv_weight)
    gap, chip = neighbours_in_pairs("dev", gap, chip)
    left = jnp.where(even != 0, gap, chip)
    right = jnp.where(even != 0, chip, gap)
    return (basis.T, smooth_edges(low, inner, high, down, up, left, right, once, twice, tv_weight))


def solution(mesh):
    placed = (P(None, "grp", "dev", None), P("grp", "dev", None), P(), P("grp", "dev", None))
    return jax.shard_map(
        on_device,
        mesh=mesh,
        in_specs=placed,
        out_specs=(P(), P(None, "grp", "dev", None)),
        check_vma=False,
    )
```

time: 72.7 us -> 69.9 us (0.961)
  waiting for transfers between devices: 5.35 us -> 1.96 us
  starting transfers between devices: 9.48 us -> 10.7 us
    ppermute x1, waiting for transfers between devices: 2.56 us -> 0.01 us  [neighbours(): lax.ppermute(toward_low, axis, [(i + 1, i) for i in range(ends)])]
    ppermute x1, waiting for transfers between devices: 1.79 us -> 0.01 us  [neighbours_in_pairs(): lax.ppermute(gap, axis, between + [(j, i) for i, j in between])]
    ppermute x1, waiting for transfers between devices: 0.01 us -> 1.29 us  [neighbours_in_pairs(): lax.ppermute(chip, axis, [(i, i ^ 1) for i in range(count)])]
    ppermute x1, starting transfers between devices: 2.27 us -> 3.51 us  [neighbours_in_pairs(): lax.ppermute(gap, axis, between + [(j, i) for i, j in between])]
    pallas_call x2 -> x4, Pallas kernels: 6.03 us -> 5.84 us  [the longest x1 1.87 us: project_inner(): pl.pallas_call(project_inner_kernel, out_shape=(jax.ShapeDtypeStruct((inn...]
  transfers between devices with their start and end apart: 4 -> 4, of which waited for: 3 -> 2; matrix products, arithmetic and copies ran while one was open for 0% -> 0% of each run, Pallas kernels for 0% -> 4%
where the time goes in v3:
time: 69.9 us; the launch traced here: 69.6 us
  blocking collectives  45.2 us (65%)
  Pallas kernels  10.8 us (15%)
  starting transfers between devices  10.7 us (15%)
  waiting for transfers between devices  1.96 us (3%)
  between operations  0.75 us (1%)
    all_to_all x1, blocking collectives, on_device(): parts = lax.all_to_all(parts, 'grp', 0, 0)  27.4 us
    all_to_all x1, blocking collectives, on_device(): parts = lax.all_to_all(parts, 'dev', 0, 0)  17.8 us
    pallas_call x1, Pallas kernels, local_grown(): pl.pallas_call(grown_kernel, out_shape=(jax.ShapeDtypeStruct((copies, 3,...  5 us
    ppermute x1, starting transfers between devices, neighbours(): lax.ppermute(toward_high, axis, [(i, i + 1) for i in range(ends)])  3.99 us
    ppermute x1, starting transfers between devices, neighbours_in_pairs(): lax.ppermute(gap, axis, between + [(j, i) for i, j in between])  3.51 us
    ppermute x1, starting transfers between devices, neighbours_in_pairs(): lax.ppermute(chip, axis, [(i, i ^ 1) for i in range(count)])  1.92 us
    pallas_call x1, Pallas kernels, project_inner(): pl.pallas_call(project_inner_kernel, out_shape=(jax.ShapeDtypeStruct((inn...  1.87 us
    pallas_call x1, Pallas kernels, project_outer(): pl.pallas_call(project_outer_kernel, out_shape=(jax.ShapeDtypeStruct((ran...  1.58 us
  transfers between devices with their start and end apart: 4, of which 2 were waited for; matrix products, arithmetic and copies ran while one was open for 0% of the time, Pallas kernels for 4%

profile of v3, /device:TPU:1, one launch (start us, length us, event | category | flops | bytes accessed | tf_op | source)
XLA Modules:
  0.0 69.6 jit_solution(6350903256446626626)
XLA Ops:
  0.6 0.0 copy-start.1
  0.6 0.0 copy-start
  0.7 5.0 %local_grown.1 = (f32[16,3,4,128]{3,2,1,0:T(4,128)S(1)}, bf16[4,192,8,256]{3,2,1,0:T(8,128)(2,1)S(1)}) custom-call(bf16[192,6,8,256]{3,2,1,0:T(8,128)(2,1)} %signals.3, s32[6,2,8]{2,1,0:T(2,128)} %bitcast.3, f32[8,192]{1,0:T(8,128)} %bitcast.6), custom_call_target="tpu_custom_call" | custom-call | tf_op jit(solution)/shard_map/local_grown/pallas_call | solution.py:133
  5.7 27.4 %all_to_all.10 = f32[16,3,4,128]{3,2,1,0:T(4,128)S(1)} all-to-all(f32[16,3,4,128]{3,2,1,0:T(4,128)S(1)} %get-tuple-element.14), channel_id=1, replica_groups=mesh['grp'=16,'dev'=32] {'grp'}, dimensions={0} | all-to-all | bytes 196608 | tf_op jit(solution)/shard_map/all_to_all | solution.py:416
  33.1 17.8 %all_to_all.11.parts = f32[32,3,4,128]{3,2,1,0:T(4,128)S(1)} all-to-all(f32[32,3,4,128]{3,2,1,0:T(4,128)S(1)} %broadcast_in_dim.15), channel_id=1, replica_groups=mesh['grp'=16,'dev'=32] {'dev'}, dimensions={0} | all-to-all | bytes 393216 | tf_op jit(solution)/shard_map/all_to_all | solution.py:419
  51.0 0.0 copy-done.1
  51.0 0.0 copy-done
  51.0 1.6 %project_outer.1 = (f32[8,192]{1,0:T(8,128)}, bf16[128,1536]{1,0:T(8,128)(2,1)S(1)}, f32[17,8,256]{2,1,0:T(8,128)S(1)}, f32[17,8,256]{2,1,0:T(8,128)S(1)}, s32[8,256]{1,0:T(8,128)S(1)}) custom-call(f32[32,3,4,128]{3,2,1,0:T(4,128)S(1)} %all_to_all.11.parts, bf16[4,192,8,256]{3,2,1,0:T(8,128)(2,1)S(1)} %get-tuple-element.15.kept, s32[6,2,8]{2,1,0:T(2,128)S(1)} %bitcast.4, ...), custom_call_target="tpu_custom_call" | custom-call | tf_op jit(solution)/shard_map/project_outer/pallas_call | solution.py:195
  52.6 1.3 %collective-permute-start.1 = (f32[17,8,256]{2,1,0:T(8,128)S(1)}, f32[17,8,256]{2,1,0:T(8,128)S(1)}, u32[]{:S(2)}, u32[]{:S(2)}) collective-permute-start(f32[17,8,256]{2,1,0:T(8,128)S(1)} %get-tuple-element.17.low), channel_id=1, source_target_pairs={{32,0},{64,32},{96,64},{128,96},{160,128},{192,160},{224,192},{256... | collective-permute-start | bytes 417800 | tf_op jit(solution)/shard_map/ppermute | solution.py:397
  53.9 4.0 %collective-permute-start = (f32[17,8,256]{2,1,0:T(8,128)S(1)}, f32[17,8,256]{2,1,0:T(8,128)S(1)}, u32[]{:S(2)}, u32[]{:S(2)}) collective-permute-start(f32[17,8,256]{2,1,0:T(8,128)S(1)} %get-tuple-element.19.high), channel_id=1, source_target_pairs={{0,32},{32,64},{64,96},{96,128},{128,160},{160,192},{192,224},{224... | collective-permute-start | bytes 417800 | tf_op jit(solution)/shard_map/ppermute | solution.py:396
  57.9 1.9 %project_inner.1 = (f32[2,8,8,256]{3,2,1,0:T(8,128)S(1)}, f32[13,8,256]{2,1,0:T(8,128)S(1)}) custom-call(bf16[192,6,8,256]{3,2,1,0:T(8,128)(2,1)} %signals.3, bf16[128,1536]{1,0:T(8,128)(2,1)S(1)} %get-tuple-element.18.mixer, s32[6,2,8]{2,1,0:T(2,128)S(1)} %bitcast.5, f32[6,8,256]{2,1,0:T(8,128)S(1)} %copy-done, f32[17,8,256]{2,1,0:T(8,128)S(1)} %get-tuple-element.17.low, ...), custom_call_target="tpu_custom_call" | custom-call | flops 1500000000 | bytes 6000000 | tf_op jit(solution)/shard_map/project_inner/pallas_call | solution.py:245
  59.7 0.0 collective-permute-done.1.up
  59.8 0.7 collective-permute-done.down
  60.4 3.5 %collective-permute-start.2 = (f32[15,8,256]{2,1,0:T(8,128)S(1)}, f32[15,8,256]{2,1,0:T(8,128)S(1)}, u32[]{:S(2)}, u32[]{:S(2)}) collective-permute-start(f32[15,8,256]{2,1,0:T(8,128)S(1)} %pad_maximum_fusion), channel_id=1, source_target_pairs={{1,2},{3,4},{5,6},{7,8},{9,10},{11,12},{13,14},{15,16},{17,18},{19... | collective-permute-start | bytes 368648 | tf_op jit(solution)/shard_map/ppermute | solution.py:405
  64.0 0.9 %smooth_middle.1 = (f32[8,6,8,256]{3,2,1,0:T(8,128)S(1)}, f32[6,4,8,256]{3,2,1,0:T(8,128)S(1)}, f32[15,8,256]{2,1,0:T(8,128)S(1)}) custom-call(f32[17,8,256]{2,1,0:T(8,128)S(1)} %get-tuple-element.17.low, f32[2,8,8,256]{3,2,1,0:T(8,128)S(1)} %get-tuple-element.20.inner, f32[17,8,256]{2,1,0:T(8,128)S(1)} %get-tuple-element.19.high, ...), custom_call_target="tpu_custom_call" | custom-call | flops 50000000 | bytes 3000000 | tf_op jit(solution)/shard_map/smooth_middle/pallas_call | solution.py:317
  64.9 1.9 %collective-permute-start.3 = (f32[15,8,256]{2,1,0:T(8,128)S(1)}, f32[15,8,256]{2,1,0:T(8,128)S(1)}, u32[]{:S(2)}, u32[]{:S(2)}) collective-permute-start(f32[15,8,256]{2,1,0:T(8,128)S(1)} %get-tuple-element.23), channel_id=1, source_target_pairs={{0,1},{1,0},{2,3},{3,2},{4,5},{5,4},{6,7},{7,6},{8,9},{9,8},{10,11... | collective-permute-start | bytes 368648 | tf_op jit(solution)/shard_map/ppermute | solution.py:406
  66.8 0.0 collective-permute-done.2
  66.8 1.3 %collective-permute-done.3 = f32[15,8,256]{2,1,0:T(8,128)S(1)} collective-permute-done((f32[15,8,256]{2,1,0:T(8,128)S(1)}, f32[15,8,256]{2,1,0:T(8,128)S(1)}, u32[]{:S(2)}, u32[]{:S(2)}) %collective-permute-start.3) | collective-permute-done | bytes 122912 | tf_op jit(solution)/shard_map/ppermute | solution.py:406
  68.2 1.5 %smooth_edges.1 = f32[8,6,8,256]{3,2,1,0:T(8,128)} custom-call(f32[17,8,256]{2,1,0:T(8,128)S(1)} %get-tuple-element.17.low, f32[2,8,8,256]{3,2,1,0:T(8,128)S(1)} %get-tuple-element.20.inner, f32[17,8,256]{2,1,0:T(8,128)S(1)} %get-tuple-element.19.high, f32[17,8,256]{2,1,0:T(8,128)S(1)} %collective-permute-done.down, ...), custom_call_target="tpu_custom_call" | custom-call | tf_op jit(solution)/shard_map/smooth_edges/pallas_call | solution.py:379
  (8 shorter events, 0.1 us)
Async XLA Ops:
  0.6 50.3 %copy-start.1 = (s32[6,8,2]{1,2,0:T(2,128)S(1)}, s32[6,8,2]{1,2,0:T(2,128)}, u32[]{:S(2)}) copy-start(s32[6,8,2]{1,2,0:T(2,128)} %param.5) | copy-start | bytes 1156
  0.6 50.3 %copy-start = (f32[6,8,256]{2,1,0:T(8,128)S(1)}, f32[6,8,256]{2,1,0:T(8,128)}, u32[]{:S(2)}) copy-start(f32[6,8,256]{2,1,0:T(8,128)} %weight.7) | copy-start | bytes 147460
  52.6 7.2 %collective-permute-start.1 = (f32[17,8,256]{2,1,0:T(8,128)S(1)}, f32[17,8,256]{2,1,0:T(8,128)S(1)}, u32[]{:S(2)}, u32[]{:S(2)}) collective-permute-start(f32[17,8,256]{2,1,0:T(8,128)S(1)} %get-tuple-element.17.low), channel_id=1, source_target_pairs={{32,0},{64,32},{96,64},{128,96},{160,128},{192,160},{224,192},{256... | collective-permute-start | bytes 417800 | tf_op jit(solution)/shard_map/ppermute | solution.py:397
  53.9 6.6 %collective-permute-start = (f32[17,8,256]{2,1,0:T(8,128)S(1)}, f32[17,8,256]{2,1,0:T(8,128)S(1)}, u32[]{:S(2)}, u32[]{:S(2)}) collective-permute-start(f32[17,8,256]{2,1,0:T(8,128)S(1)} %get-tuple-element.19.high), channel_id=1, source_target_pairs={{0,32},{32,64},{64,96},{96,128},{128,160},{160,192},{192,224},{224... | collective-permute-start | bytes 417800 | tf_op jit(solution)/shard_map/ppermute | solution.py:396
  60.4 6.4 %collective-permute-start.2 = (f32[15,8,256]{2,1,0:T(8,128)S(1)}, f32[15,8,256]{2,1,0:T(8,128)S(1)}, u32[]{:S(2)}, u32[]{:S(2)}) collective-permute-start(f32[15,8,256]{2,1,0:T(8,128)S(1)} %pad_maximum_fusion), channel_id=1, source_target_pairs={{1,2},{3,4},{5,6},{7,8},{9,10},{11,12},{13,14},{15,16},{17,18},{19... | collective-permute-start | bytes 368648 | tf_op jit(solution)/shard_map/ppermute | solution.py:405
  64.9 3.2 %collective-permute-start.3 = (f32[15,8,256]{2,1,0:T(8,128)S(1)}, f32[15,8,256]{2,1,0:T(8,128)S(1)}, u32[]{:S(2)}, u32[]{:S(2)}) collective-permute-start(f32[15,8,256]{2,1,0:T(8,128)S(1)} %get-tuple-element.23), channel_id=1, source_target_pairs={{0,1},{1,0},{2,3},{3,2},{4,5},{5,4},{6,7},{7,6},{8,9},{9,8},{10,11... | collective-permute-start | bytes 368648 | tf_op jit(solution)/shard_map/ppermute | solution.py:406

commit v4 on v3

--- a/solution.py
+++ b/solution.py
@@ -157,8 +157,7 @@
         pivot = grown[k : k + 1]
         inner = jnp.sum(grown * pivot, axis=1, keepdims=True)
         norm2 = inner[k : k + 1]
-        scaled = pivot * (1.0 / norm2)
-        grown = jnp.where(row > k, grown - inner * scaled, grown)
+        grown = jnp.where(row > k, grown - (inner / norm2) * pivot, grown)
         grown = jnp.where(row == k, pivot / jnp.sqrt(norm2), grown)
     return grown
 
@@ -208,7 +207,7 @@
     )(parts, kept, flags, tv_weight)
 
 
-def project_inner_kernel(signals, mixer, flags, weight, low, high, inner, gap, planes, sems):
+def project_inner_kernel(signals, mixer, flags, weight, low, high, inner, chip, gap, planes, sems):
     frames, count, rows, width = signals.shape
     copies = [
         pltpu.make_async_copy(signals.at[:, x], planes.at[i], sems.at[i]) for i, x in enumerate(inner_planes(count))
@@ -221,13 +220,16 @@
 
     def edges(x, head, tail):
         for y in range(2):
+            chip[y * count + x] = jnp.where(even, tail[y], head[y])
             gap[y * count + x] = jnp.where(even, head[y], tail[y])
 
     for i, x in enumerate(outer_planes(count)):
         face, first = (low if i < 2 else high), (i % 2) * rows
         edges(x, face[first : first + 2], face[first + rows - 2 : first + rows])
     blank = jnp.zeros((rank - count, width), jnp.float32)
+    chip[2 * count, :count] = jnp.where(even, weight[:, rows - 1], weight[:, 0])
     gap[2 * count, :count] = jnp.where(even, weight[:, 0], weight[:, rows - 1])
+    chip[2 * count, count:] = blank
     gap[2 * count, count:] = blank
     for i, x in enumerate(inner_planes(count)):
         copies[i].wait()
@@ -244,9 +246,9 @@
     vmem = pl.BlockSpec(memory_space=pltpu.VMEM)
     return pl.pallas_call(
         project_inner_kernel,
-        out_shape=(jax.ShapeDtypeStruct((inner, size_y, rank, size_z), jnp.float32), edge),
+        out_shape=(jax.ShapeDtypeStruct((inner, size_y, rank, size_z), jnp.float32), edge, edge),
         in_specs=[pl.BlockSpec(memory_space=pltpu.HBM)] + [vmem] * 5,
-        out_specs=(vmem,) * 2,
+        out_specs=(vmem,) * 3,
         scratch_shapes=[
             pltpu.VMEM((inner, frames, size_y, size_z), signals.dtype),
             pltpu.SemaphoreType.DMA((inner,)),
@@ -284,18 +286,9 @@
     return faces[0] + faces[1] + [inner.at[i] for i in range(inner.shape[0])] + faces[2] + faces[3]
 
 
-def smooth_middle_kernel(low, inner, high, down, up, weight, once, twice, chip):
+def smooth_middle_kernel(low, inner, high, down, up, weight, once, twice):
     count, rows, width = weight.shape
-    rank = low.shape[1]
     planes = x_planes(low, inner, high, down, up)
-    even = (lax.axis_index("dev") & 1) == 0
-    for x in range(count):
-        for y in range(2):
-            chip[y * count + x] = jnp.where(even, planes[x + 2][rows - 2 + y], planes[x + 2][y])
-    chip[2 * count, :count] = jnp.where(even, weight[:, rows - 1], weight[:, 0])
-    chip[2 * count, count:] = jnp.zeros((rank - count, width), jnp.float32)
-    for i, plane in enumerate((planes[1], planes[count + 2])):
-        chip[2 * count + 1 + i] = jnp.where(even, plane[rows - 1], plane[0])
     weights = [down.at[2 * rows]] + [weight.at[x] for x in range(count)] + [up.at[2 * rows]]
     size = rows - 2
     before = slope(planes[1][1 : 1 + size] - planes[0][1 : 1 + size])
@@ -319,10 +312,9 @@
         out_shape=(
             jax.ShapeDtypeStruct((count + 2, rows - 2, rank, width), jnp.float32),
             jax.ShapeDtypeStruct((count, rows - 4, rank, width), jnp.float32),
-            jax.ShapeDtypeStruct((2 * count + 3, rank, width), jnp.float32),
         ),
         in_specs=[vmem] * 6,
-        out_specs=(vmem,) * 3,
+        out_specs=(vmem,) * 2,
         compiler_params=pltpu.CompilerParams(vmem_limit_bytes=limit),
         cost_estimate=pl.CostEstimate(flops=50000000, bytes_accessed=3000000, transcendentals=1000000),
         name="smooth_middle",
@@ -412,21 +404,22 @@
     rank = basis_old.shape[1]
     flags = jnp.transpose(tile_flags, (0, 2, 1))
     pinned = [pltpu.with_memory_space_constraint(a, pltpu.HBM) for a in (signals, flags, basis_old.T)]
-    parts, kept = local_grown(*pinned, lax.axis_size("grp"))
+    parts, kept = local_grown(*pinned, lax.axis_size("dev"))
+    parts = lax.all_to_all(parts, "dev", 0, 0)
+    summed = jnp.sum(parts, axis=0)
+    parts = jnp.broadcast_to(summed[None], (lax.axis_size("grp"),) + summed.shape)
     parts = lax.all_to_all(parts, "grp", 0, 0)
-    summed = jnp.sum(parts, axis=0)
-    parts = jnp.broadcast_to(summed[None], (lax.axis_size("dev"),) + summed.shape)
-    parts = lax.all_to_all(parts, "dev", 0, 0)
     basis, mixer, low, high, even = project_outer(parts, kept, flags, tv_weight, rank)
     down, up = neighbours("grp", low, high)
-    inner, gap = project_inner(pinned[0], mixer, flags, tv_weight, low, high)
+    inner, chip, gap = project_inner(pinned[0], mixer, flags, tv_weight, low, high)
     heads = jnp.stack([down[size_y], up[0]])
     tails = jnp.stack([down[2 * size_y - 1], up[size_y - 1]])
+    chip = jnp.concatenate([chip, jnp.where(even != 0, tails, heads)], axis=0)
     gap = jnp.concatenate([gap, jnp.where(even != 0, heads, tails)], axis=0)
-    once, twice, chip = smooth_middle(low, inner, high, down, up, tv_weight)
     gap, chip = neighbours_in_pairs("dev", gap, chip)
-    left = jnp.where(even != 0, gap, chip)
-    right = jnp.where(even != 0, chip, gap)
+    once, twice = smooth_middle(low, inner, high, down, up, tv_weight)
+    left = jnp.where(even == 0, chip, gap)
+    right = jnp.where(even == 0, gap, chip)
     return (basis.T, smooth_edges(low, inner, high, down, up, left, right, once, twice, tv_weight))
 
 

time: 69.9 us -> 69.2 us (0.990); the launches traced: 69.6 us -> 68 us
  blocking collectives: 45.2 us -> 43.4 us
  starting transfers between devices: 10.7 us -> 12.5 us
  waiting for transfers between devices: 1.96 us -> 0.45 us
    all_to_all x1, blocking collectives: 27.4 us -> 25.5 us  [on_device(): parts = lax.all_to_all(parts, 'grp', 0, 0)]
    ppermute x1, starting transfers between devices: 3.51 us -> 5.27 us  [neighbours_in_pairs(): lax.ppermute(gap, axis, between + [(j, i) for i, j in between])]
    ppermute x1, waiting for transfers between devices: 1.29 us -> 0.36 us  [neighbours_in_pairs(): lax.ppermute(chip, axis, [(i, i ^ 1) for i in range(count)])]
where the time goes in v4:
time: 69.2 us; the launch traced here: 68 us
  blocking collectives  43.4 us (63%)
  starting transfers between devices  12.5 us (18%)
  Pallas kernels  10.8 us (16%)
  between operations  0.76 us (1%)
    all_to_all x1, blocking collectives, on_device(): parts = lax.all_to_all(parts, 'grp', 0, 0)  25.5 us
    all_to_all x1, blocking collectives, on_device(): parts = lax.all_to_all(parts, 'dev', 0, 0)  17.9 us
    ppermute x1, starting transfers between devices, neighbours_in_pairs(): lax.ppermute(gap, axis, between + [(j, i) for i, j in between])  5.27 us
    pallas_call x1, Pallas kernels, local_grown(): pl.pallas_call(grown_kernel, out_shape=(jax.ShapeDtypeStruct((copies, 3,...  5.01 us
    ppermute x1, starting transfers between devices, neighbours(): lax.ppermute(toward_high, axis, [(i, i + 1) for i in range(ends)])  3.99 us
    ppermute x1, starting transfers between devices, neighbours_in_pairs(): lax.ppermute(chip, axis, [(i, i ^ 1) for i in range(count)])  1.92 us
    pallas_call x1, Pallas kernels, project_inner(): pl.pallas_call(project_inner_kernel, out_shape=(jax.ShapeDtypeStruct((inn...  1.88 us
    pallas_call x1, Pallas kernels, project_outer(): pl.pallas_call(project_outer_kernel, out_shape=(jax.ShapeDtypeStruct((ran...  1.56 us
  transfers between devices with their start and end apart: 4, of which 2 were waited for; matrix products, arithmetic and copies ran while one was open for 0% of the time, Pallas kernels for 4%

profile of v4, /device:TPU:1, one launch (start us, length us, event | category | flops | bytes accessed | tf_op | source)
XLA Modules:
  0.0 68.0 jit_solution(16763471727909118001)
XLA Ops:
  0.6 0.0 copy-start.1
  0.6 0.0 copy-start
  0.7 5.0 %local_grown.1 = (f32[32,3,4,128]{3,2,1,0:T(4,128)S(1)}, bf16[4,192,8,256]{3,2,1,0:T(8,128)(2,1)S(1)}) custom-call(bf16[192,6,8,256]{3,2,1,0:T(8,128)(2,1)} %signals.3, s32[6,2,8]{2,1,0:T(2,128)} %bitcast.3, f32[8,192]{1,0:T(8,128)} %bitcast.6), custom_call_target="tpu_custom_call" | custom-call | tf_op jit(solution)/shard_map/local_grown/pallas_call | solution.py:133
  5.7 17.9 %all_to_all.10 = f32[32,3,4,128]{3,2,1,0:T(4,128)S(1)} all-to-all(f32[32,3,4,128]{3,2,1,0:T(4,128)S(1)} %get-tuple-element.14), channel_id=1, replica_groups=mesh['grp'=16,'dev'=32] {'dev'}, dimensions={0} | all-to-all | bytes 393216 | tf_op jit(solution)/shard_map/all_to_all | solution.py:408
  23.6 0.1 reduce_sum.9
  23.6 25.5 %all_to_all.11.parts = f32[16,3,4,128]{3,2,1,0:T(4,128)S(1)} all-to-all(f32[16,3,4,128]{3,2,1,0:T(4,128)S(1)} %broadcast_in_dim.16), channel_id=1, replica_groups=mesh['grp'=16,'dev'=32] {'grp'}, dimensions={0} | all-to-all | bytes 196608 | tf_op jit(solution)/shard_map/all_to_all | solution.py:411
  49.1 0.0 copy-done.1
  49.1 0.0 copy-done
  49.1 1.6 %project_outer.1 = (f32[8,192]{1,0:T(8,128)}, bf16[128,1536]{1,0:T(8,128)(2,1)S(1)}, f32[17,8,256]{2,1,0:T(8,128)S(1)}, f32[17,8,256]{2,1,0:T(8,128)S(1)}, s32[8,256]{1,0:T(8,128)S(1)}) custom-call(f32[16,3,4,128]{3,2,1,0:T(4,128)S(1)} %all_to_all.11.parts, bf16[4,192,8,256]{3,2,1,0:T(8,128)(2,1)S(1)} %get-tuple-element.15.kept, s32[6,2,8]{2,1,0:T(2,128)S(1)} %bitcast.4, ...), custom_call_target="tpu_custom_call" | custom-call | tf_op jit(solution)/shard_map/project_outer/pallas_call | solution.py:194
  50.7 1.3 %collective-permute-start.1 = (f32[17,8,256]{2,1,0:T(8,128)S(1)}, f32[17,8,256]{2,1,0:T(8,128)S(1)}, u32[]{:S(2)}, u32[]{:S(2)}) collective-permute-start(f32[17,8,256]{2,1,0:T(8,128)S(1)} %get-tuple-element.17.low), channel_id=1, source_target_pairs={{32,0},{64,32},{96,64},{128,96},{160,128},{192,160},{224,192},{256... | collective-permute-start | bytes 417800 | tf_op jit(solution)/shard_map/ppermute | solution.py:389
  52.0 4.0 %collective-permute-start = (f32[17,8,256]{2,1,0:T(8,128)S(1)}, f32[17,8,256]{2,1,0:T(8,128)S(1)}, u32[]{:S(2)}, u32[]{:S(2)}) collective-permute-start(f32[17,8,256]{2,1,0:T(8,128)S(1)} %get-tuple-element.19.high), channel_id=1, source_target_pairs={{0,32},{32,64},{64,96},{96,128},{128,160},{160,192},{192,224},{224... | collective-permute-start | bytes 417800 | tf_op jit(solution)/shard_map/ppermute | solution.py:388
  56.0 1.9 %project_inner.1 = (f32[2,8,8,256]{3,2,1,0:T(8,128)S(1)}, f32[13,8,256]{2,1,0:T(8,128)S(1)}, f32[13,8,256]{2,1,0:T(8,128)S(1)}) custom-call(bf16[192,6,8,256]{3,2,1,0:T(8,128)(2,1)} %signals.3, bf16[128,1536]{1,0:T(8,128)(2,1)S(1)} %get-tuple-element.18.mixer, s32[6,2,8]{2,1,0:T(2,128)S(1)} %bitcast.5, f32[6,8,256]{2,1,0:T(8,128)S(1)} %copy-done, ...), custom_call_target="tpu_custom_call" | custom-call | flops 1500000000 | bytes 6000000 | tf_op jit(solution)/shard_map/project_inner/pallas_call | solution.py:247
  57.9 0.0 collective-permute-done.1.up
  57.9 0.1 collective-permute-done.down
  58.0 5.3 %collective-permute-start.3 = (f32[15,8,256]{2,1,0:T(8,128)S(1)}, f32[15,8,256]{2,1,0:T(8,128)S(1)}, u32[]{:S(2)}, u32[]{:S(2)}) collective-permute-start(f32[15,8,256]{2,1,0:T(8,128)S(1)} %pad_maximum_fusion.1), channel_id=1, source_target_pairs={{1,2},{3,4},{5,6},{7,8},{9,10},{11,12},{13,14},{15,16},{17,18},{19... | collective-permute-start | bytes 368648 | tf_op jit(solution)/shard_map/ppermute | solution.py:397
  63.3 1.9 %collective-permute-start.2 = (f32[15,8,256]{2,1,0:T(8,128)S(1)}, f32[15,8,256]{2,1,0:T(8,128)S(1)}, u32[]{:S(2)}, u32[]{:S(2)}) collective-permute-start(f32[15,8,256]{2,1,0:T(8,128)S(1)} %pad_maximum_fusion), channel_id=1, source_target_pairs={{0,1},{1,0},{2,3},{3,2},{4,5},{5,4},{6,7},{7,6},{8,9},{9,8},{10,11... | collective-permute-start | bytes 368648 | tf_op jit(solution)/shard_map/ppermute | solution.py:398
  65.2 0.9 %smooth_middle.1 = (f32[8,6,8,256]{3,2,1,0:T(8,128)S(1)}, f32[6,4,8,256]{3,2,1,0:T(8,128)S(1)}) custom-call(f32[17,8,256]{2,1,0:T(8,128)S(1)} %get-tuple-element.17.low, f32[2,8,8,256]{3,2,1,0:T(8,128)S(1)} %get-tuple-element.20.inner, f32[17,8,256]{2,1,0:T(8,128)S(1)} %get-tuple-element.19.high, f32[17,8,256]{2,1,0:T(8,128)S(1)} %collective-permute-done.down, ...), custom_call_target="tpu_custom_call" | custom-call | flops 50000000 | bytes 3000000 | tf_op jit(solution)/shard_map/smooth_middle/pallas_call | solution.py:310
  66.2 0.0 collective-permute-done.3
  66.2 0.4 collective-permute-done.2
  66.6 1.5 %smooth_edges.1 = f32[8,6,8,256]{3,2,1,0:T(8,128)} custom-call(f32[17,8,256]{2,1,0:T(8,128)S(1)} %get-tuple-element.17.low, f32[2,8,8,256]{3,2,1,0:T(8,128)S(1)} %get-tuple-element.20.inner, f32[17,8,256]{2,1,0:T(8,128)S(1)} %get-tuple-element.19.high, f32[17,8,256]{2,1,0:T(8,128)S(1)} %collective-permute-done.down, ...), custom_call_target="tpu_custom_call" | custom-call | tf_op jit(solution)/shard_map/smooth_edges/pallas_call | solution.py:371
  (8 shorter events, 0.1 us)
Async XLA Ops:
  0.6 48.5 %copy-start.1 = (s32[6,8,2]{1,2,0:T(2,128)S(1)}, s32[6,8,2]{1,2,0:T(2,128)}, u32[]{:S(2)}) copy-start(s32[6,8,2]{1,2,0:T(2,128)} %param.5) | copy-start | bytes 1156
  0.6 48.5 %copy-start = (f32[6,8,256]{2,1,0:T(8,128)S(1)}, f32[6,8,256]{2,1,0:T(8,128)}, u32[]{:S(2)}) copy-start(f32[6,8,256]{2,1,0:T(8,128)} %weight.7) | copy-start | bytes 147460
  50.7 7.2 %collective-permute-start.1 = (f32[17,8,256]{2,1,0:T(8,128)S(1)}, f32[17,8,256]{2,1,0:T(8,128)S(1)}, u32[]{:S(2)}, u32[]{:S(2)}) collective-permute-start(f32[17,8,256]{2,1,0:T(8,128)S(1)} %get-tuple-element.17.low), channel_id=1, source_target_pairs={{32,0},{64,32},{96,64},{128,96},{160,128},{192,160},{224,192},{256... | collective-permute-start | bytes 417800 | tf_op jit(solution)/shard_map/ppermute | solution.py:389
  52.0 6.0 %collective-permute-start = (f32[17,8,256]{2,1,0:T(8,128)S(1)}, f32[17,8,256]{2,1,0:T(8,128)S(1)}, u32[]{:S(2)}, u32[]{:S(2)}) collective-permute-start(f32[17,8,256]{2,1,0:T(8,128)S(1)} %get-tuple-element.19.high), channel_id=1, source_target_pairs={{0,32},{32,64},{64,96},{96,128},{128,160},{160,192},{192,224},{224... | collective-permute-start | bytes 417800 | tf_op jit(solution)/shard_map/ppermute | solution.py:388
  58.0 8.2 %collective-permute-start.3 = (f32[15,8,256]{2,1,0:T(8,128)S(1)}, f32[15,8,256]{2,1,0:T(8,128)S(1)}, u32[]{:S(2)}, u32[]{:S(2)}) collective-permute-start(f32[15,8,256]{2,1,0:T(8,128)S(1)} %pad_maximum_fusion.1), channel_id=1, source_target_pairs={{1,2},{3,4},{5,6},{7,8},{9,10},{11,12},{13,14},{15,16},{17,18},{19... | collective-permute-start | bytes 368648 | tf_op jit(solution)/shard_map/ppermute | solution.py:397
  63.3 3.2 %collective-permute-start.2 = (f32[15,8,256]{2,1,0:T(8,128)S(1)}, f32[15,8,256]{2,1,0:T(8,128)S(1)}, u32[]{:S(2)}, u32[]{:S(2)}) collective-permute-start(f32[15,8,256]{2,1,0:T(8,128)S(1)} %pad_maximum_fusion), channel_id=1, source_target_pairs={{0,1},{1,0},{2,3},{3,2},{4,5},{5,4},{6,7},{7,6},{8,9},{9,8},{10,11... | collective-permute-start | bytes 368648 | tf_op jit(solution)/shard_map/ppermute | solution.py:398

commit v5 on v4

--- a/solution.py
+++ b/solution.py
@@ -280,6 +280,15 @@
     return cells + step_size * weight[:, None, :] * total, after
 
 
+def update_planes(field, first, count, weight):
+    stop = first + count
+    cells = field[first:stop, 1:3]
+    along_x = slope(field[first : stop + 1, 1:3] - field[first - 1 : stop, 1:3])
+    along_y = slope(field[first:stop, 1:4] - field[first:stop, 0:3])
+    total = (along_x[1:] - along_x[:-1]) + (along_y[:, 1:] - along_y[:, :-1]) + along_z(cells)
+    return cells + step_size * weight[:, :, None, :] * total
+
+
 def x_planes(low, inner, high, down, up):
     rows = inner.shape[1]
     faces = [[face.at[:rows], face.at[rows : 2 * rows]] for face in (down, low, high, up)]
@@ -300,7 +309,8 @@
     before = slope(planes[1][1 : 1 + size] - planes[0][1 : 1 + size])
     for i in range(1, count + 1):
         fresh, before = update(planes, i, 1, size, before, weight[i - 1, 2 : 2 + size])
-        twice[i - 1] = fresh
+        for y in range(size):
+            twice[:, i - 1, 2 + y] = fresh[y]
 
 
 def smooth_middle(low, inner, high, down, up, tv_weight):
@@ -311,7 +321,7 @@
         smooth_middle_kernel,
         out_shape=(
             jax.ShapeDtypeStruct((count + 2, rows - 2, rank, width), jnp.float32),
-            jax.ShapeDtypeStruct((count, rows - 4, rank, width), jnp.float32),
+            jax.ShapeDtypeStruct((rank, count, rows, width), jnp.float32),
         ),
         in_specs=[vmem] * 6,
         out_specs=(vmem,) * 2,
@@ -325,9 +335,7 @@
     count, rows, width = weight.shape
     planes = x_planes(low, inner, high, down, up)
     last = len(planes) - 1
-    for x in range(count):
-        for y in range(2, rows - 2):
-            out[:, x, y] = twice[x, y - 2]
+    out[...] = twice[...]
     for side, received in enumerate((left, right)):
         edge = 1 if side else 2
         mine, theirs, shift = (0, 2, 2) if side else (2, 0, 0)
@@ -344,24 +352,21 @@
         before = slope(cells[1][edge : edge + 1] - cells[0][edge : edge + 1])
         fresh, _ = update(cells, 1, edge, 1, before, down[2 * rows, outer : outer + 1])
         fresher[side, 0, shift + edge - 1] = fresh[0]
-        before = slope(cells[2][1:3] - cells[1][1:3])
-        for x in range(count):
-            pair = [weight[x, outer : outer + 1], received[2 * count, x : x + 1]]
-            pair = jnp.concatenate(pair if side else pair[::-1], axis=0)
-            fresh, before = update(cells, x + 2, 1, 2, before, pair)
-            fresher[side, x + 1, shift : shift + 2] = fresh
-        before = before[edge - 1 : edge]
+        near = received[2 * count, :count][:, None, :]
+        pair = [weight[:, outer : outer + 1], near]
+        pair = jnp.concatenate(pair if side else pair[::-1], axis=1)
+        fresher[side, 1 : count + 1, shift : shift + 2] = update_planes(field.at[side], 2, count, pair)
+        before = slope(cells[last - 1][edge : edge + 1] - cells[last - 2][edge : edge + 1])
         fresh, _ = update(cells, last - 1, edge, 1, before, up[2 * rows, outer : outer + 1])
         fresher[side, count + 1, shift + edge - 1] = fresh[0]
         done = slice(rows - 4, rows - 2) if side else slice(0, 2)
         cells = [fresher.at[side, i] for i in range(count + 2)]
         for i in range(count + 2):
             cells[i][2 - shift : 4 - shift] = once[i, done]
-        before = slope(cells[1][1:3] - cells[0][1:3])
+        fresh = update_planes(fresher.at[side], 1, count, weight[:, own])
         for x in range(count):
-            fresh, before = update(cells, x + 1, 1, 2, before, weight[x, own])
             for y in range(2):
-                out[:, x, own.start + y] = fresh[y]
+                out[:, x, own.start + y] = fresh[x, y]
 
 
 def smooth_edges(low, inner, high, down, up, left, right, once, twice, tv_weight):

time: 69.2 us -> 69.2 us (level)
  no operation moved by 1% of the time
where the time goes in v5:
time: 69.2 us; the launch traced here: 67.9 us
  blocking collectives  43.4 us (63%)
  starting transfers between devices  12.5 us (18%)
  Pallas kernels  10.8 us (16%)
  between operations  0.76 us (1%)
    all_to_all x1, blocking collectives, on_device(): parts = lax.all_to_all(parts, 'grp', 0, 0)  25.5 us
    all_to_all x1, blocking collectives, on_device(): parts = lax.all_to_all(parts, 'dev', 0, 0)  17.9 us
    ppermute x1, starting transfers between devices, neighbours_in_pairs(): lax.ppermute(gap, axis, between + [(j, i) for i, j in between])  5.27 us
    pallas_call x1, Pallas kernels, local_grown(): pl.pallas_call(grown_kernel, out_shape=(jax.ShapeDtypeStruct((copies, 3,...  5.01 us
    ppermute x1, starting transfers between devices, neighbours(): lax.ppermute(toward_high, axis, [(i, i + 1) for i in range(ends)])  3.99 us
    ppermute x1, starting transfers between devices, neighbours_in_pairs(): lax.ppermute(chip, axis, [(i, i ^ 1) for i in range(count)])  1.92 us
    pallas_call x1, Pallas kernels, project_inner(): pl.pallas_call(project_inner_kernel, out_shape=(jax.ShapeDtypeStruct((inn...  1.88 us
    pallas_call x1, Pallas kernels, project_outer(): pl.pallas_call(project_outer_kernel, out_shape=(jax.ShapeDtypeStruct((ran...  1.56 us
  transfers between devices with their start and end apart: 4, of which 2 were waited for; matrix products, arithmetic and copies ran while one was open for 0% of the time, Pallas kernels for 4%

profile of v5, /device:TPU:1, one launch (start us, length us, event | category | flops | bytes accessed | tf_op | source)
XLA Modules:
  0.0 67.9 jit_solution(16212017758902362474)
XLA Ops:
  0.6 0.0 copy-start.1
  0.6 0.0 copy-start
  0.7 5.0 %local_grown.1 = (f32[32,3,4,128]{3,2,1,0:T(4,128)S(1)}, bf16[4,192,8,256]{3,2,1,0:T(8,128)(2,1)S(1)}) custom-call(bf16[192,6,8,256]{3,2,1,0:T(8,128)(2,1)} %signals.3, s32[6,2,8]{2,1,0:T(2,128)} %bitcast.3, f32[8,192]{1,0:T(8,128)} %bitcast.6), custom_call_target="tpu_custom_call" | custom-call | tf_op jit(solution)/shard_map/local_grown/pallas_call | solution.py:133
  5.7 17.9 %all_to_all.10 = f32[32,3,4,128]{3,2,1,0:T(4,128)S(1)} all-to-all(f32[32,3,4,128]{3,2,1,0:T(4,128)S(1)} %get-tuple-element.14), channel_id=1, replica_groups=mesh['grp'=16,'dev'=32] {'dev'}, dimensions={0} | all-to-all | bytes 393216 | tf_op jit(solution)/shard_map/all_to_all | solution.py:413
  23.6 0.1 reduce_sum.9
  23.6 25.5 %all_to_all.11.parts = f32[16,3,4,128]{3,2,1,0:T(4,128)S(1)} all-to-all(f32[16,3,4,128]{3,2,1,0:T(4,128)S(1)} %broadcast_in_dim.16), channel_id=1, replica_groups=mesh['grp'=16,'dev'=32] {'grp'}, dimensions={0} | all-to-all | bytes 196608 | tf_op jit(solution)/shard_map/all_to_all | solution.py:416
  49.1 0.0 copy-done.1
  49.1 0.0 copy-done
  49.1 1.6 %project_outer.1 = (f32[8,192]{1,0:T(8,128)}, bf16[128,1536]{1,0:T(8,128)(2,1)S(1)}, f32[17,8,256]{2,1,0:T(8,128)S(1)}, f32[17,8,256]{2,1,0:T(8,128)S(1)}, s32[8,256]{1,0:T(8,128)S(1)}) custom-call(f32[16,3,4,128]{3,2,1,0:T(4,128)S(1)} %all_to_all.11.parts, bf16[4,192,8,256]{3,2,1,0:T(8,128)(2,1)S(1)} %get-tuple-element.15.kept, s32[6,2,8]{2,1,0:T(2,128)S(1)} %bitcast.4, ...), custom_call_target="tpu_custom_call" | custom-call | tf_op jit(solution)/shard_map/project_outer/pallas_call | solution.py:194
  50.7 1.3 %collective-permute-start.1 = (f32[17,8,256]{2,1,0:T(8,128)S(1)}, f32[17,8,256]{2,1,0:T(8,128)S(1)}, u32[]{:S(2)}, u32[]{:S(2)}) collective-permute-start(f32[17,8,256]{2,1,0:T(8,128)S(1)} %get-tuple-element.17.low), channel_id=1, source_target_pairs={{32,0},{64,32},{96,64},{128,96},{160,128},{192,160},{224,192},{256... | collective-permute-start | bytes 417800 | tf_op jit(solution)/shard_map/ppermute | solution.py:394
  52.0 4.0 %collective-permute-start = (f32[17,8,256]{2,1,0:T(8,128)S(1)}, f32[17,8,256]{2,1,0:T(8,128)S(1)}, u32[]{:S(2)}, u32[]{:S(2)}) collective-permute-start(f32[17,8,256]{2,1,0:T(8,128)S(1)} %get-tuple-element.19.high), channel_id=1, source_target_pairs={{0,32},{32,64},{64,96},{96,128},{128,160},{160,192},{192,224},{224... | collective-permute-start | bytes 417800 | tf_op jit(solution)/shard_map/ppermute | solution.py:393
  56.0 1.9 %project_inner.1 = (f32[2,8,8,256]{3,2,1,0:T(8,128)S(1)}, f32[13,8,256]{2,1,0:T(8,128)S(1)}, f32[13,8,256]{2,1,0:T(8,128)S(1)}) custom-call(bf16[192,6,8,256]{3,2,1,0:T(8,128)(2,1)} %signals.3, bf16[128,1536]{1,0:T(8,128)(2,1)S(1)} %get-tuple-element.18.mixer, s32[6,2,8]{2,1,0:T(2,128)S(1)} %bitcast.5, f32[6,8,256]{2,1,0:T(8,128)S(1)} %copy-done, ...), custom_call_target="tpu_custom_call" | custom-call | flops 1500000000 | bytes 6000000 | tf_op jit(solution)/shard_map/project_inner/pallas_call | solution.py:247
  57.9 0.0 collective-permute-done.1.up
  57.9 0.1 collective-permute-done.down
  58.0 5.3 %collective-permute-start.3 = (f32[15,8,256]{2,1,0:T(8,128)S(1)}, f32[15,8,256]{2,1,0:T(8,128)S(1)}, u32[]{:S(2)}, u32[]{:S(2)}) collective-permute-start(f32[15,8,256]{2,1,0:T(8,128)S(1)} %pad_maximum_fusion.1), channel_id=1, source_target_pairs={{1,2},{3,4},{5,6},{7,8},{9,10},{11,12},{13,14},{15,16},{17,18},{19... | collective-permute-start | bytes 368648 | tf_op jit(solution)/shard_map/ppermute | solution.py:402
  63.3 1.9 %collective-permute-start.2 = (f32[15,8,256]{2,1,0:T(8,128)S(1)}, f32[15,8,256]{2,1,0:T(8,128)S(1)}, u32[]{:S(2)}, u32[]{:S(2)}) collective-permute-start(f32[15,8,256]{2,1,0:T(8,128)S(1)} %pad_maximum_fusion), channel_id=1, source_target_pairs={{0,1},{1,0},{2,3},{3,2},{4,5},{5,4},{6,7},{7,6},{8,9},{9,8},{10,11... | collective-permute-start | bytes 368648 | tf_op jit(solution)/shard_map/ppermute | solution.py:403
  65.2 0.9 %smooth_middle.1 = (f32[8,6,8,256]{3,2,1,0:T(8,128)S(1)}, f32[8,6,8,256]{3,2,1,0:T(8,128)S(1)}) custom-call(f32[17,8,256]{2,1,0:T(8,128)S(1)} %get-tuple-element.17.low, f32[2,8,8,256]{3,2,1,0:T(8,128)S(1)} %get-tuple-element.20.inner, f32[17,8,256]{2,1,0:T(8,128)S(1)} %get-tuple-element.19.high, f32[17,8,256]{2,1,0:T(8,128)S(1)} %collective-permute-done.down, ...), custom_call_target="tpu_custom_call" | custom-call | flops 50000000 | bytes 3000000 | tf_op jit(solution)/shard_map/smooth_middle/pallas_call | solution.py:320
  66.2 0.0 collective-permute-done.3
  66.2 0.3 collective-permute-done.2
  66.6 1.4 %smooth_edges.1 = f32[8,6,8,256]{3,2,1,0:T(8,128)} custom-call(f32[17,8,256]{2,1,0:T(8,128)S(1)} %get-tuple-element.17.low, f32[2,8,8,256]{3,2,1,0:T(8,128)S(1)} %get-tuple-element.20.inner, f32[17,8,256]{2,1,0:T(8,128)S(1)} %get-tuple-element.19.high, f32[17,8,256]{2,1,0:T(8,128)S(1)} %collective-permute-done.down, ...), custom_call_target="tpu_custom_call" | custom-call | tf_op jit(solution)/shard_map/smooth_edges/pallas_call | solution.py:376
  (8 shorter events, 0.1 us)
Async XLA Ops:
  0.6 48.5 %copy-start.1 = (s32[6,8,2]{1,2,0:T(2,128)S(1)}, s32[6,8,2]{1,2,0:T(2,128)}, u32[]{:S(2)}) copy-start(s32[6,8,2]{1,2,0:T(2,128)} %param.5) | copy-start | bytes 1156
  0.6 48.5 %copy-start = (f32[6,8,256]{2,1,0:T(8,128)S(1)}, f32[6,8,256]{2,1,0:T(8,128)}, u32[]{:S(2)}) copy-start(f32[6,8,256]{2,1,0:T(8,128)} %weight.7) | copy-start | bytes 147460
  50.7 7.2 %collective-permute-start.1 = (f32[17,8,256]{2,1,0:T(8,128)S(1)}, f32[17,8,256]{2,1,0:T(8,128)S(1)}, u32[]{:S(2)}, u32[]{:S(2)}) collective-permute-start(f32[17,8,256]{2,1,0:T(8,128)S(1)} %get-tuple-element.17.low), channel_id=1, source_target_pairs={{32,0},{64,32},{96,64},{128,96},{160,128},{192,160},{224,192},{256... | collective-permute-start | bytes 417800 | tf_op jit(solution)/shard_map/ppermute | solution.py:394
  52.0 6.0 %collective-permute-start = (f32[17,8,256]{2,1,0:T(8,128)S(1)}, f32[17,8,256]{2,1,0:T(8,128)S(1)}, u32[]{:S(2)}, u32[]{:S(2)}) collective-permute-start(f32[17,8,256]{2,1,0:T(8,128)S(1)} %get-tuple-element.19.high), channel_id=1, source_target_pairs={{0,32},{32,64},{64,96},{96,128},{128,160},{160,192},{192,224},{224... | collective-permute-start | bytes 417800 | tf_op jit(solution)/shard_map/ppermute | solution.py:393
  58.0 8.2 %collective-permute-start.3 = (f32[15,8,256]{2,1,0:T(8,128)S(1)}, f32[15,8,256]{2,1,0:T(8,128)S(1)}, u32[]{:S(2)}, u32[]{:S(2)}) collective-permute-start(f32[15,8,256]{2,1,0:T(8,128)S(1)} %pad_maximum_fusion.1), channel_id=1, source_target_pairs={{1,2},{3,4},{5,6},{7,8},{9,10},{11,12},{13,14},{15,16},{17,18},{19... | collective-permute-start | bytes 368648 | tf_op jit(solution)/shard_map/ppermute | solution.py:402
  63.3 3.2 %collective-permute-start.2 = (f32[15,8,256]{2,1,0:T(8,128)S(1)}, f32[15,8,256]{2,1,0:T(8,128)S(1)}, u32[]{:S(2)}, u32[]{:S(2)}) collective-permute-start(f32[15,8,256]{2,1,0:T(8,128)S(1)} %pad_maximum_fusion), channel_id=1, source_target_pairs={{0,1},{1,0},{2,3},{3,2},{4,5},{5,4},{6,7},{7,6},{8,9},{9,8},{10,11... | collective-permute-start | bytes 368648 | tf_op jit(solution)/shard_map/ppermute | solution.py:403
